TPU v7x, 256 devices: a whole 4x4x8 slice. The times are simulated.
256 devices in a mesh: attn: 32 (over z, x), tensor: 8 (over y, core).
Axes of the slice: x: 4, y: 4, z: 8, core: 2. Of those that a mesh axis runs over, the one named last changes fastest.
Arguments:
- queries: bfloat16 [32, 8192], P('attn', 'tensor'), may hold values from -4.5 to 4.5
- fresh_keys: bfloat16 [32, 1024], P('attn', 'tensor'), may hold values from -10 to 10
- fresh_values: bfloat16 [32, 1024], P('attn', 'tensor'), may hold values from -6 to 6
- key_cache_blocks: bfloat16 [1024, 512, 1024], P('attn', None, 'tensor'), may hold values from -100 to 100
- value_cache_blocks: bfloat16 [1024, 512, 1024], P('attn', None, 'tensor'), may hold values from -6 to 6
- lengths: int32 [32], replicated, may hold values from 2 to 127488, as said below
- placement: int32 [32, 249], replicated, may hold values from -1 to 1023, as said below
- w_out: bfloat16 [8192, 8192], P('tensor', 'attn'), may hold values from -0.0625 to 0.0625
Outputs:
- projected: bfloat16 [32, 8192], P(None, ('attn', 'tensor'))
Inputs may be any that keep to these rules, and one draw needn't show every extreme that they name: A row's cache takes ceil(lengths / 512) blocks, at most 249; all rows together take at most 1024 blocks. `placement`: entry j of row r names the block (index along attn times 32 plus slot) holding the row's tokens j * 512 to (j + 1) * 512 - 1 for j < ceil(lengths[r] / 512), and is -1 beyond; no block is named twice.
All inputs are finite; a program needn't handle non-finite values.
Results may differ from a plain program's by a relative error of at most 0.0075.
Values may be sent and summed in bfloat16 or wider, within the bound.
No kernel may reach another device: no remote copies, remote signals or barrier semaphores. Data moves between devices by JAX's collectives and lax.ppermute only.
A program may use at most 64 MiB of HBM per device.

v0:
```python
import math

import jax
import jax.numpy as jnp
from jax import lax
from jax.sharding import PartitionSpec as P

QUERY_HEADS = 64
KEY_VALUE_HEADS = 8
HEAD_SIZE = 128


def finish(all_peaks, masses, all_sums, self_score, own_values):
    highest = jnp.maximum(jnp.max(all_peaks, axis=0), self_score)
    factor = jnp.exp(all_peaks - highest[None])
    own_weight = jnp.exp(self_score - highest)
    denominator = jnp.sum(masses * factor, axis=0) + own_weight
    blended_draw = jnp.sum(all_sums * factor[..., None], axis=0)
    blended_draw = (
        blended_draw + own_weight.astype(jnp.bfloat16).astype(jnp.float32)[..., None] * own_values
    )
    return blended_draw / denominator[..., None]


def shards(
    queries,
    fresh_keys,
    fresh_values,
    key_cache_blocks,
    value_cache_blocks,
    lengths,
    placement,
    w_out,
):
    own_rows, q_width = queries.shape
    slot_count, block_len, kv_width = key_cache_blocks.shape
    kv_local = kv_width // HEAD_SIZE
    group_width = QUERY_HEADS // KEY_VALUE_HEADS
    head_local = kv_local * group_width
    logit_scale = 1.0 / math.sqrt(HEAD_SIZE)
    every_query = lax.all_gather(queries, "attn", axis=0, tiled=True)
    row_count = every_query.shape[0]
    slot_ids = lax.axis_index("attn") * slot_count + jnp.arange(slot_count, dtype=jnp.int32)
    matches = placement[:, :, None] == slot_ids[None, None, :]
    slot_owner = jnp.any(matches, axis=1)
    block_index = jnp.arange(placement.shape[1], dtype=jnp.int32)
    slot_block = jnp.sum(jnp.where(matches, block_index[None, :, None], 0), axis=(0, 1))
    slot_length = jnp.sum(jnp.where(slot_owner, lengths[:, None], 0), axis=0)
    live_count = jnp.clip(slot_length - slot_block * block_len, 0, block_len)
    one_hot = slot_owner.T.astype(jnp.float32)
    slot_query = jnp.dot(
        one_hot.astype(jnp.bfloat16), every_query, preferred_element_type=jnp.float32
    ).astype(jnp.bfloat16)
    query_blocks = slot_query.reshape(slot_count, kv_local, group_width, HEAD_SIZE)
    key_blocks = key_cache_blocks.reshape(slot_count, block_len, kv_local, HEAD_SIZE)
    value_blocks = value_cache_blocks.reshape(slot_count, block_len, kv_local, HEAD_SIZE)
    scores = (
        jnp.einsum("skgd,stkd->skgt", query_blocks, key_blocks, preferred_element_type=jnp.float32)
        * logit_scale
    )
    is_live = (jnp.arange(block_len, dtype=jnp.int32)[None, :] < live_count[:, None])[
        :, None, None, :
    ]
    slot_peak = jnp.max(jnp.where(is_live, scores, -1e30), axis=-1)
    weights = jnp.where(is_live, jnp.exp(scores - slot_peak[..., None]), 0.0)
    slot_mass = jnp.sum(weights, axis=-1).reshape(slot_count, head_local)
    slot_sum = jnp.einsum(
        "skgt,stkd->skgd",
        weights.astype(jnp.bfloat16),
        value_blocks,
        preferred_element_type=jnp.float32,
    )
    slot_sum = slot_sum.reshape(slot_count, head_local, HEAD_SIZE)
    slot_peak = slot_peak.reshape(slot_count, head_local)
    row_peak = jnp.max(jnp.where(slot_owner.T[:, :, None], slot_peak[:, None, :], -1e30), axis=0)
    slot_top = jnp.dot(one_hot, row_peak, precision=lax.Precision.HIGHEST)
    factor = jnp.exp(slot_peak - slot_top)
    row_mass = jnp.dot(one_hot.T, slot_mass * factor, precision=lax.Precision.HIGHEST)
    scaled_sum = (slot_sum * factor[..., None]).reshape(slot_count, head_local * HEAD_SIZE)
    row_sum = jnp.dot(one_hot.T, scaled_sum, precision=lax.Precision.HIGHEST).reshape(
        row_count, head_local, HEAD_SIZE
    )
    own_query = queries.reshape(own_rows, kv_local, group_width, HEAD_SIZE)
    self_score = jnp.einsum(
        "rkgd,rkd->rkg",
        own_query,
        fresh_keys.reshape(own_rows, kv_local, HEAD_SIZE),
        preferred_element_type=jnp.float32,
    )
    self_score = (self_score * logit_scale).reshape(own_rows, head_local)
    own_values = jnp.broadcast_to(
        fresh_values.reshape(own_rows, kv_local, 1, HEAD_SIZE),
        (own_rows, kv_local, group_width, HEAD_SIZE),
    )
    own_values = own_values.reshape(own_rows, head_local, HEAD_SIZE).astype(jnp.float32)
    all_peaks, masses, all_sums = (
        lax.all_to_all(row_peak[None], "attn", split_axis=1, concat_axis=0, tiled=True),
        lax.all_to_all(row_mass[None], "attn", split_axis=1, concat_axis=0, tiled=True),
        lax.all_to_all(row_sum[None], "attn", split_axis=1, concat_axis=0, tiled=True),
    )
    attended = (
        finish(all_peaks, masses, all_sums, self_score, own_values)
        .reshape(own_rows, q_width)
        .astype(jnp.bfloat16)
    )
    partial_out = jnp.dot(
        lax.all_gather(attended, "attn", axis=0, tiled=True),
        w_out,
        preferred_element_type=jnp.float32,
    )
    return lax.psum_scatter(partial_out, "tensor", scatter_dimension=1, tiled=True).astype(
        jnp.bfloat16
    )


def solution(mesh):
    return jax.shard_map(
        shards,
        mesh=mesh,
        in_specs=(
            P("attn", "tensor"),
            P("attn", "tensor"),
            P("attn", "tensor"),
            P("attn", None, "tensor"),
            P("attn", None, "tensor"),
            P(),
            P(),
            P("tensor", "attn"),
        ),
        out_specs=P(None, ("attn", "tensor")),
        check_vma=False,
    )
```

profile of v0, /device:TPU:1, one launch (start us, length us, event | category | flops | bytes accessed | tf_op | source)
XLA Modules:
  0.0 185.0 jit_solution(639424146059503811)
XLA Ops:
  6.5 0.0 copy-start
  6.5 0.0 copy-start.2
  6.5 1.5 compare_reduce_fusion
  8.1 1.1 fusion.3
  9.1 0.8 select_reduce_fusion.2
  9.9 0.1 iota_compare_fusion
  10.0 37.1 %all-gather = bf16[32,1,1024]{2,1,0:T(2,128)(2,1)S(1)} all-gather(bf16[1,1,1024]{2,1,0:T(2,128)(2,1)} %bitcast.99), channel_id=1, replica_groups=mesh['attn'=32,'tensor'=8] {'attn'}, dimensions={0}, use_global_device_ids=true | all-gather | bytes 67584 | tf_op jit(solution)/shard_map/all_gather | solution.py:41
  47.0 0.2 fusion
  47.2 0.1 copy.25
  47.3 0.0 copy-start.1
  47.3 3.5 %select_reduce_fusion = (f32[32,8]{1,0:T(8,128)S(1)}, f32[32,8,512]{2,1,0:T(8,128)S(1)}) fusion(pred[32,512]{1,0:T(8,128)(4,1)S(1)} %iota_compare_fusion, bf16[32,8,128]{2,1,0:T(8,128)(2,1)S(1)} %bitcast.88, bf16[32,512,128]{2,1,0:T(8,128)(2,1)} %param.11), kind=kOutput, calls=%fused_computation.14 | convolution fusion | flops 33947392 | bytes 4801536 | tf_op jit(solution)/shard_map/skgd,stkd->skgt/dot_general | solution.py:58
  50.8 0.0 copy-start.3
  50.8 0.1 select_reduce_fusion.1
  50.9 0.7 copy.30
  51.6 6.1 %all-to-all-start.1 = ((f32[1,32,8]{2,0,1:T(1,128)}), f32[1,32,8]{2,0,1:T(1,128)S(1)}, u32[]{:S(2)}, u32[]{:S(2)}) async-start(f32[1,32,8]{2,0,1:T(1,128)} %copy.30), calls=%async_computation.1 | async-start | bytes 32768 | tf_op jit(solution)/shard_map/all_to_all | solution.py:97
  57.7 0.1 copy.26
  57.8 0.3 fusion.4
  58.0 0.1 copy.31
  58.1 0.1 fusion.1
  58.2 0.1 copy.27
  58.3 0.8 fusion.21
  59.1 0.0 copy-done.2
  59.1 2.9 %convolution_multiply_fusion.1 = f32[32,8,128]{2,1,0:T(8,128)S(1)} fusion(bf16[32,512,128]{2,1,0:T(8,128)(2,1)} %param.12, f32[32,8,512]{2,1,0:T(8,128)S(1)} %get-tuple-element.8, f32[32,8]{1,0:T(8,128)S(1)} %get-tuple-element.7, pred[32,512]{1,0:T(8,128)(4,1)S(1)} %iota_compare_fusion, f32[32,8]{1,0:T(8,128)S(1)} %copy.27), kind=kOutput, calls=%fused_computation.4 | convolution fusion | flops 33980416 | bytes 4868096 | tf_op jit(solution)/shard_map/skgt,stkd->skgd/dot_general | solution.py:67
  62.0 0.2 convolution_bitcast_fusion.1
  62.2 0.0 copy-done.1
  62.2 0.7 copy.29
  63.0 3.2 %all-to-all-done.1 = f32[1,32,8]{2,0,1:T(1,128)S(1)} async-done(((f32[1,32,8]{2,0,1:T(1,128)}), f32[1,32,8]{2,0,1:T(1,128)S(1)}, u32[]{:S(2)}, u32[]{:S(2)}) %all-to-all-start.1) | async-done | bytes 1056 | tf_op jit(solution)/shard_map/all_to_all | solution.py:97
  66.2 6.0 %all-to-all-start.2 = ((f32[1,32,8]{2,0,1:T(1,128)}), f32[1,32,8]{2,0,1:T(1,128)S(1)}, u32[]{:S(2)}, u32[]{:S(2)}) async-start(f32[1,32,8]{2,0,1:T(1,128)} %bitcast.26), calls=%async_computation.2 | async-start | bytes 32768 | tf_op jit(solution)/shard_map/all_to_all | solution.py:98
  72.2 0.1 reduce_max.29
  72.2 0.0 copy-done.3
  72.2 0.1 convert_convert_fusion.2
  72.4 8.4 %all-to-all-done.2 = f32[1,32,8]{2,0,1:T(1,128)S(1)} async-done(((f32[1,32,8]{2,0,1:T(1,128)}), f32[1,32,8]{2,0,1:T(1,128)S(1)}, u32[]{:S(2)}, u32[]{:S(2)}) %all-to-all-start.2) | async-done | bytes 1056 | tf_op jit(solution)/shard_map/all_to_all | solution.py:98
  80.8 3.9 %all-to-all-start = ((f32[1,32,8,128]{3,2,0,1:T(8,128)}), f32[1,32,8,128]{3,2,0,1:T(8,128)S(1)}, u32[]{:S(2)}, u32[]{:S(2)}) async-start(f32[1,32,8,128]{3,2,0,1:T(8,128)} %copy.29), calls=%async_computation | async-start | bytes 262144 | tf_op jit(solution)/shard_map/all_to_all | solution.py:99
  84.6 0.0 reduce-scatter.4.cloned.1.call-start
  84.7 9.3 %all-to-all-done = f32[1,32,8,128]{3,2,0,1:T(8,128)S(1)} async-done(((f32[1,32,8,128]{3,2,0,1:T(8,128)}), f32[1,32,8,128]{3,2,0,1:T(8,128)S(1)}, u32[]{:S(2)}, u32[]{:S(2)}) %all-to-all-start) | async-done | bytes 131104 | tf_op jit(solution)/shard_map/all_to_all | solution.py:99
  94.0 0.1 fusion.12
  94.1 0.1 div.20
  94.2 0.1 mul.94
  94.3 32.1 %all-gather.1 = bf16[32,1,1024]{2,1,0:T(2,128)(2,1)S(1)} all-gather(bf16[1,1,1024]{2,1,0:T(2,128)(2,1)S(1)} %convert_bitcast_fusion), channel_id=1, replica_groups=mesh['attn'=32,'tensor'=8] {'attn'}, dimensions={0}, use_global_device_ids=true | all-gather | bytes 67584 | tf_op jit(solution)/shard_map/all_gather | solution.py:107
  126.4 0.0 copy-done
  126.4 1.0 convolution_bitcast_fusion
  127.4 0.0 reduce-scatter.4.cloned.1.call-update
  127.4 49.4 %reduce-scatter.4.cloned.1.call-done = f32[32,32]{1,0:T(8,128)} async-done(((f32[256,32]{1,0:T(8,128)}), f32[32,32]{1,0:T(8,128)}) %reduce-scatter.4.cloned.1.call-update) | async-done | bytes 4112
  176.8 1.4 copy.34
  (10 shorter events, 0.1 us)
Async XLA Ops:
  6.5 119.9 %copy-start = (bf16[1024,256]{1,0:T(8,128)(2,1)S(1)}, bf16[1024,256]{1,0:T(8,128)(2,1)}, u32[]{:S(2)}) copy-start(bf16[1024,256]{1,0:T(8,128)(2,1)} %param.15) | copy-start | bytes 1572868
  6.5 52.5 %copy-start.2 = (bf16[1,128]{1,0:T(2,128)(2,1)S(1)}, bf16[1,128]{1,0:T(2,128)(2,1)}, u32[]{:S(2)}) copy-start(bf16[1,128]{1,0:T(2,128)(2,1)} %param.10) | copy-start | bytes 772
  47.3 14.9 %copy-start.1 = (bf16[1,1024]{1,0:T(2,128)(2,1)S(1)}, bf16[1,1024]{1,0:T(2,128)(2,1)}, u32[]{:S(2)}) copy-start(bf16[1,1024]{1,0:T(2,128)(2,1)} %param.8) | copy-start | bytes 6148
  50.8 21.4 %copy-start.3 = (bf16[1,128]{1,0:T(2,128)(2,1)S(1)}, bf16[1,128]{1,0:T(2,128)(2,1)}, u32[]{:S(2)}) copy-start(bf16[1,128]{1,0:T(2,128)(2,1)} %param.9) | copy-start | bytes 772
  51.6 14.6 %all-to-all-start.1 = ((f32[1,32,8]{2,0,1:T(1,128)}), f32[1,32,8]{2,0,1:T(1,128)S(1)}, u32[]{:S(2)}, u32[]{:S(2)}) async-start(f32[1,32,8]{2,0,1:T(1,128)} %copy.30), calls=%async_computation.1 | async-start | bytes 32768 | tf_op jit(solution)/shard_map/all_to_all | solution.py:97
  66.2 14.6 %all-to-all-start.2 = ((f32[1,32,8]{2,0,1:T(1,128)}), f32[1,32,8]{2,0,1:T(1,128)S(1)}, u32[]{:S(2)}, u32[]{:S(2)}) async-start(f32[1,32,8]{2,0,1:T(1,128)} %bitcast.26), calls=%async_computation.2 | async-start | bytes 32768 | tf_op jit(solution)/shard_map/all_to_all | solution.py:98
  80.8 13.3 %all-to-all-start = ((f32[1,32,8,128]{3,2,0,1:T(8,128)}), f32[1,32,8,128]{3,2,0,1:T(8,128)S(1)}, u32[]{:S(2)}, u32[]{:S(2)}) async-start(f32[1,32,8,128]{3,2,0,1:T(8,128)} %copy.29), calls=%async_computation | async-start | bytes 262144 | tf_op jit(solution)/shard_map/all_to_all | solution.py:99
  84.6 92.2 %reduce-scatter.4.cloned.1.call-start = ((), (), s32[]{:S(2)}) async-start(), calls=%async_computation.4 | async-start | bytes 147456
Sparse Core Ops, SparseCore 0:
  127.5 49.1 reduce-scatter.3
where the time goes:
time: 187 us; the launch traced here: 185 us
  waiting for transfers between devices  70.3 us (38%)
  blocking collectives  69.2 us (37%)
  starting transfers between devices  16 us (9%)
  between operations  13.5 us (7%)
  matrix products  8.74 us (5%)
  other arithmetic  4.03 us (2%)
  local copies, waits for them, and re-layouts  3.25 us (2%)
    unnamed x2, waiting for transfers between devices  49.4 us
    all_gather x1, blocking collectives, shards(): every_query = lax.all_gather(queries, 'attn', axis=0, tiled=True)  37.1 us
    all_gather x1, blocking collectives, shards(): lax.all_gather(attended, 'attn', axis=0, tiled=True)  32.1 us
    all_to_all x1, waiting for transfers between devices, shards(): lax.all_to_all(row_sum[None], 'attn', split_axis=1, concat_axis=0, tiled=...  9.3 us
    all_to_all x1, waiting for transfers between devices, shards(): lax.all_to_all(row_mass[None], 'attn', split_axis=1, concat_axis=0, tiled...  8.42 us
    all_to_all x1, starting transfers between devices, shards(): lax.all_to_all(row_peak[None], 'attn', split_axis=1, concat_axis=0, tiled...  6.13 us
    all_to_all x1, starting transfers between devices, shards(): lax.all_to_all(row_mass[None], 'attn', split_axis=1, concat_axis=0, tiled...  6.02 us
    all_to_all x1, starting transfers between devices, shards(): lax.all_to_all(row_sum[None], 'attn', split_axis=1, concat_axis=0, tiled=...  3.85 us
  transfers between devices with their start and end apart: 4, of which 4 were waited for; matrix products, arithmetic and copies ran while one was open for 3% of the time, Pallas kernels for 0%

commit v1 on v0

v1 whole, which is shorter than its diff:
```python
import math

import jax
import jax.numpy as jnp
from jax import lax
from jax.experimental import pallas as pl
from jax.experimental.pallas import tpu as pltpu
from jax.sharding import PartitionSpec as P

QUERY_HEADS = 64
KEY_VALUE_HEADS = 8
HEAD_SIZE = 128
GROUP = QUERY_HEADS // KEY_VALUE_HEADS
SCALE = 1.0 / math.sqrt(HEAD_SIZE)
LOW = -1e30
LIVE_BITS = 10

VMEM = pl.BlockSpec(memory_space=pltpu.VMEM)
SMEM = pl.BlockSpec(memory_space=pltpu.SMEM)


def slots_kernel(first_ref, lengths_ref, placement_ref, code_ref):
    places = placement_ref[...] - first_ref[0]
    row = lax.broadcasted_iota(jnp.int32, places.shape, 0)
    start = lax.broadcasted_iota(jnp.int32, places.shape, 1) * 512
    live = jnp.clip(lengths_ref[...] - start, 0, 512)
    code = row * (1 << LIVE_BITS) + live
    for slot in range(code_ref.shape[0]):
        code_ref[slot] = jnp.sum(jnp.where(places == slot, code, 0))


def attention_kernel(code_ref, query_ref, key_ref, value_ref, out_ref, scores, peaks, masses, sums):
    slots, block, _ = key_ref.shape
    rows = query_ref.shape[0]
    contract_last = (((1,), (1,)), ((), ()))
    position = lax.broadcasted_iota(jnp.int32, (GROUP, block), 1)
    peaks[...] = jnp.full_like(peaks, LOW)
    masses[...] = jnp.zeros_like(masses)
    sums[...] = jnp.zeros_like(sums)
    for slot in range(slots):
        code = code_ref[slot]
        row = code >> LIVE_BITS
        live = code & ((1 << LIVE_BITS) - 1)
        s = lax.dot_general(
            query_ref[row], key_ref[slot], contract_last, preferred_element_type=jnp.float32
        )
        s = jnp.where(position < live, s * SCALE, LOW)
        scores[slot] = s
        top = s[:, :128]
        for part in range(1, block // 128):
            top = jnp.maximum(top, s[:, part * 128 : (part + 1) * 128])
        peaks[row] = jnp.maximum(peaks[row], top)
    top = jnp.max(peaks[...], axis=-1, keepdims=True)
    top = top.astype(jnp.bfloat16).astype(jnp.float32)
    peaks[...] = jnp.broadcast_to(top, peaks.shape)
    for slot in range(slots):
        code = code_ref[slot]
        row = code >> LIVE_BITS
        live = code & ((1 << LIVE_BITS) - 1)
        w = jnp.exp(scores[slot] - jnp.tile(peaks[row], (1, block // 128)))
        w = jnp.where(position < live, w, 0.0)
        mass = w[:, :128]
        for part in range(1, block // 128):
            mass = mass + w[:, part * 128 : (part + 1) * 128]
        masses[row] = masses[row] + mass
        sums[row] = sums[row] + jnp.dot(
            w.astype(jnp.bfloat16), value_ref[slot], preferred_element_type=jnp.float32
        )
    mass = jnp.sum(masses[...], axis=-1, keepdims=True)
    high = mass.astype(jnp.bfloat16).astype(jnp.float32)
    lane = lax.broadcasted_iota(jnp.int32, (rows, GROUP, 128), 2)
    extra = jnp.where(lane == 0, peaks[...], jnp.where(lane == 1, high, mass - high))
    out_ref[...] = jnp.concatenate([sums[...], extra], axis=1).astype(jnp.bfloat16)


def finish_kernel(parts_ref, query_ref, key_ref, value_ref, out_ref):
    parts = parts_ref[...].astype(jnp.float32)
    partial = parts[:, :GROUP]
    extra = parts[:, GROUP:]
    own = jnp.sum(
        query_ref[0].astype(jnp.float32) * key_ref[...].astype(jnp.float32), axis=-1, keepdims=True
    )
    own = own * SCALE
    peaks = extra[:, :, 0:1]
    highest = jnp.maximum(jnp.max(peaks, axis=0), own)
    factor = jnp.exp(peaks - highest[None])
    own_weight = jnp.exp(own - highest)
    masses = extra[:, :, 1:2] + extra[:, :, 2:3]
    denominator = jnp.sum(masses * factor, axis=0) + own_weight
    total = jnp.sum(partial * factor, axis=0)
    total = total + own_weight.astype(jnp.bfloat16).astype(jnp.float32) * value_ref[...].astype(
        jnp.float32
    )
    attended = (total / denominator).astype(jnp.bfloat16)
    out_ref[...] = jnp.broadcast_to(attended[None], out_ref.shape)


def project_kernel(attended_ref, w_ref, out_ref):
    heads = jnp.swapaxes(attended_ref[...].astype(jnp.float32), 0, 1).astype(jnp.bfloat16)
    total = None
    for head in range(GROUP):
        term = jnp.dot(
            heads[head],
            w_ref[head * HEAD_SIZE : (head + 1) * HEAD_SIZE, :],
            preferred_element_type=jnp.float32,
        )
        total = term if total is None else total + term
    width = out_ref.shape[2]
    for part in range(out_ref.shape[0]):
        out_ref[part] = total[:, part * width : (part + 1) * width]


def shards(
    queries,
    fresh_keys,
    fresh_values,
    key_cache_blocks,
    value_cache_blocks,
    lengths,
    placement,
    w_out,
):
    rows = lengths.shape[0]
    slots = key_cache_blocks.shape[0]
    first = (lax.axis_index("attn") * slots).astype(jnp.int32).reshape(1)
    codes = pl.pallas_call(
        slots_kernel,
        out_shape=jax.ShapeDtypeStruct((slots,), jnp.int32),
        in_specs=[SMEM, VMEM, VMEM],
        out_specs=SMEM,
        name="slots",
    )(first, lengths.reshape(rows, 1), placement)

    own_query = queries.reshape(1, GROUP, HEAD_SIZE)
    every_query = lax.all_to_all(
        jnp.broadcast_to(own_query, (rows, GROUP, HEAD_SIZE)), "attn", 0, 0, tiled=True
    )
    state = pltpu.VMEM((rows, GROUP, 128), jnp.float32)
    partials = pl.pallas_call(
        attention_kernel,
        out_shape=jax.ShapeDtypeStruct((rows, 2 * GROUP, HEAD_SIZE), jnp.bfloat16),
        in_specs=[SMEM, VMEM, VMEM, VMEM],
        out_specs=VMEM,
        scratch_shapes=[pltpu.VMEM((slots, GROUP, key_cache_blocks.shape[1]), jnp.float32), state, state, state],
        name="attention",
    )(codes, every_query, key_cache_blocks, value_cache_blocks)
    partials = lax.all_to_all(partials, "attn", 0, 0, tiled=True)
    attended = pl.pallas_call(
        finish_kernel,
        out_shape=jax.ShapeDtypeStruct((rows, GROUP, HEAD_SIZE), jnp.bfloat16),
        in_specs=[VMEM] * 4,
        out_specs=VMEM,
        name="finish",
    )(partials, own_query, fresh_keys, fresh_values)
    attended = lax.all_to_all(attended, "attn", 0, 0, tiled=True)
    ranks = lax.axis_size("tensor")
    terms = pl.pallas_call(
        project_kernel,
        out_shape=jax.ShapeDtypeStruct((ranks, rows, w_out.shape[1] // ranks), jnp.float32),
        in_specs=[VMEM] * 2,
        out_specs=VMEM,
        name="project",
    )(attended, w_out)
    terms = lax.all_to_all(terms, "tensor", 0, 0, tiled=True)
    return jnp.sum(terms, axis=0).astype(jnp.bfloat16)


def solution(mesh):
    return jax.shard_map(
        shards,
        mesh=mesh,
        in_specs=(
            P("attn", "tensor"),
            P("attn", "tensor"),
            P("attn", "tensor"),
            P("attn", None, "tensor"),
            P("attn", None, "tensor"),
            P(),
            P(),
            P("tensor", "attn"),
        ),
        out_specs=P(None, ("attn", "tensor")),
        check_vma=False,
    )
```

time: 187 us -> 76.9 us (0.41)
  waiting for transfers between devices: 70.3 us -> 5.82 us
  blocking collectives: 69.2 us -> 40.8 us
  between operations: 13.5 us -> 0.05 us
  Pallas kernels: 0 us -> 11.6 us
  matrix products: 8.74 us -> 0 us
  starting transfers between devices: 16 us -> 11.9 us
  other arithmetic: 4.03 us -> 2.04 us
    all_gather x2 -> x0, blocking collectives: 69.2 us -> none  [the longest x1 37.1 us: shards(): every_query = lax.all_gather(queries, 'attn', axis=0, tiled=True)]
    unnamed x2 -> x0, waiting for transfers between devices: 49.4 us -> none
    all_to_all x0 -> x3, blocking collectives: none -> 40.8 us  [the longest x1 13.9 us: shards(): partials = lax.all_to_all(partials, 'attn', 0, 0, tiled=True)]
    all_to_all x3 -> x1, waiting for transfers between devices: 20.9 us -> 5.82 us  [shards(): lax.all_to_all(jnp.broadcast_to(own_query, (rows, GROUP, HEAD_SIZE)), 'at...]
    pallas_call x0 -> x4, Pallas kernels: none -> 11.6 us  [the longest x1 6.14 us: shards(): pl.pallas_call(attention_kernel, out_shape=jax.ShapeDtypeStruct((rows, 2...]
    dot_general x7 -> x0, matrix products: 7.75 us -> none  [the longest x1 3.47 us: shards(): jnp.einsum('skgd,stkd->skgt', query_blocks, key_blocks, preferred_element...]
    all_to_all x3 -> x1, starting transfers between devices: 16 us -> 11.9 us  [shards(): lax.all_to_all(jnp.broadcast_to(own_query, (rows, GROUP, HEAD_SIZE)), 'at...]
  transfers between devices with their start and end apart: 4 -> 1, of which waited for: 4 -> 1; matrix products, arithmetic and copies ran while one was open for 3% -> 2% of each run, Pallas kernels for 0% -> 2%
where the time goes in v1:
time: 76.9 us; the launch traced here: 76.4 us
  blocking collectives  40.8 us (53%)
  starting transfers between devices  11.9 us (15%)
  Pallas kernels  11.6 us (15%)
  waiting for transfers between devices  5.82 us (8%)
  local copies, waits for them, and re-layouts  4.21 us (5%)
  other arithmetic  2.04 us (3%)
    all_to_all x1, blocking collectives, shards(): partials = lax.all_to_all(partials, 'attn', 0, 0, tiled=True)  13.9 us
    all_to_all x1, blocking collectives, shards(): terms = lax.all_to_all(terms, 'tensor', 0, 0, tiled=True)  13.4 us
    all_to_all x1, blocking collectives, shards(): attended = lax.all_to_all(attended, 'attn', 0, 0, tiled=True)  13.4 us
    all_to_all x1, starting transfers between devices, shards(): lax.all_to_all(jnp.broadcast_to(own_query, (rows, GROUP, HEAD_SIZE)), 'at...  11.9 us
    pallas_call x1, Pallas kernels, shards(): pl.pallas_call(attention_kernel, out_shape=jax.ShapeDtypeStruct((rows, 2...  6.14 us
    all_to_all x1, waiting for transfers between devices, shards(): lax.all_to_all(jnp.broadcast_to(own_query, (rows, GROUP, HEAD_SIZE)), 'at...  5.82 us
    pallas_call x1, Pallas kernels, shards(): pl.pallas_call(project_kernel, out_shape=jax.ShapeDtypeStruct((ranks, row...  2 us
    pallas_call x1, Pallas kernels, shards(): pl.pallas_call(finish_kernel, out_shape=jax.ShapeDtypeStruct((rows, GROUP...  1.82 us
  transfers between devices with their start and end apart: 1, of which 1 were waited for; matrix products, arithmetic and copies ran while one was open for 2% of the time, Pallas kernels for 2%

profile of v1, /device:TPU:1, one launch (start us, length us, event | category | flops | bytes accessed | tf_op | source)
XLA Modules:
  0.0 76.4 jit_solution(4385933628770306227)
XLA Ops:
  0.0 0.7 reduce
  0.7 0.0 copy-start.1
  0.7 0.6 broadcast_in_dim.8
  1.3 11.9 %all-to-all-start = ((bf16[32,8,128]{2,1,0:T(8,128)(2,1)}), bf16[32,8,128]{2,1,0:T(8,128)(2,1)S(1)}, u32[]{:S(2)}, u32[]{:S(2)}) async-start(bf16[32,8,128]{2,1,0:T(8,128)(2,1)} %broadcast_in_dim.8), calls=%async_computation | async-start | bytes 131072 | tf_op jit(solution)/shard_map/all_to_all | solution.py:135
  13.2 1.3 %copy.9.lengths_ref = s32[32,1]{1,0:T(8,128)} copy(s32[32,1]{0,1:T(1,128)} %bitcast.6) | data formatting | bytes 256 | tf_op jit(solution)/shard_map/reshape | solution.py:132
  14.6 1.6 %slots.1.code_ref = s32[32]{0:T(128)} custom-call(s32[1]{0:T(128)} %bitcast.first_ref, s32[32,1]{1,0:T(8,128)} %copy.9.lengths_ref, s32[32,249]{1,0:T(8,128)} %placement_ref.1), custom_call_target="tpu_custom_call" | custom-call | tf_op jit(solution)/shard_map/slots/pallas_call | solution.py:126
  16.2 5.8 %all-to-all-done.query_ref = bf16[32,8,128]{2,1,0:T(8,128)(2,1)S(1)} async-done(((bf16[32,8,128]{2,1,0:T(8,128)(2,1)}), bf16[32,8,128]{2,1,0:T(8,128)(2,1)S(1)}, u32[]{:S(2)}, u32[]{:S(2)}) %all-to-all-start) | async-done | bytes 65568 | tf_op jit(solution)/shard_map/all_to_all | solution.py:135
  22.0 0.0 copy-start
  22.0 0.6 copy-done
  22.7 6.1 %attention.1 = bf16[32,16,128]{2,1,0:T(8,128)(2,1)} custom-call(s32[32]{0:T(128)} %slots.1.code_ref, bf16[32,8,128]{2,1,0:T(8,128)(2,1)} %copy-done, bf16[32,512,128]{2,1,0:T(8,128)(2,1)} %key_ref.2, bf16[32,512,128]{2,1,0:T(8,128)(2,1)} %value_ref.2), custom_call_target="tpu_custom_call" | custom-call | tf_op jit(solution)/shard_map/attention/pallas_call | solution.py:139
  28.8 0.0 copy-done.1
  28.8 13.9 %all_to_all.20.parts_ref = bf16[32,16,128]{2,1,0:T(8,128)(2,1)} all-to-all(bf16[32,16,128]{2,1,0:T(8,128)(2,1)} %attention.1), channel_id=1, replica_groups=mesh['attn'=32,'tensor'=8] {'attn'}, dimensions={0} | all-to-all | bytes 262144 | tf_op jit(solution)/shard_map/all_to_all | solution.py:147
  42.7 1.8 %finish.1 = bf16[32,8,128]{2,1,0:T(8,128)(2,1)} custom-call(bf16[32,16,128]{2,1,0:T(8,128)(2,1)} %all_to_all.20.parts_ref, bf16[1,8,128]{2,1,0:T(8,128)(2,1)} %bitcast.5, bf16[1,128]{1,0:T(2,128)(2,1)} %key_ref.3, bf16[1,128]{1,0:T(2,128)(2,1)} %value_ref.3), custom_call_target="tpu_custom_call" | custom-call | tf_op jit(solution)/shard_map/finish/pallas_call | solution.py:148
  44.6 13.4 %all_to_all.21.attended_ref = bf16[32,8,128]{2,1,0:T(8,128)(2,1)} all-to-all(bf16[32,8,128]{2,1,0:T(8,128)(2,1)} %finish.1), channel_id=1, replica_groups=mesh['attn'=32,'tensor'=8] {'attn'}, dimensions={0} | all-to-all | bytes 131072 | tf_op jit(solution)/shard_map/all_to_all | solution.py:155
  58.0 2.0 %project.1 = f32[8,32,32]{2,1,0:T(8,128)} custom-call(bf16[32,8,128]{2,1,0:T(8,128)(2,1)} %all_to_all.21.attended_ref, bf16[1024,256]{1,0:T(8,128)(2,1)} %w_ref.1), custom_call_target="tpu_custom_call" | custom-call | tf_op jit(solution)/shard_map/project/pallas_call | solution.py:157
  60.0 1.0 %reshape.15 = f32[8,1,1024]{2,1,0:T(1,128)S(1)} reshape(f32[8,32,32]{2,1,0:T(8,128)} %project.1) | data formatting | bytes 65536
  61.0 13.4 %all_to_all.22 = f32[8,1,1024]{2,1,0:T(1,128)S(1)} all-to-all(f32[8,1,1024]{2,1,0:T(1,128)S(1)} %reshape.15), channel_id=1, replica_groups=mesh['attn'=32,'tensor'=8] {'tensor'}, dimensions={0} | all-to-all | bytes 65536 | tf_op jit(solution)/shard_map/all_to_all | solution.py:164
  74.4 0.5 broadcast.2
  74.9 0.7 reduce.2
  75.7 0.1 reshape.16
  75.8 0.6 reduce_sum.9
Async XLA Ops:
  0.7 28.1 %copy-start.1 = (bf16[1024]{0:T(1024)(128)(2,1)}, bf16[1024]{0:T(1024)(128)(2,1)S(1)}, u32[]{:S(2)}) copy-start(bf16[1024]{0:T(1024)(128)(2,1)S(1)} %reduce) | copy-start | bytes 6148
  1.3 20.7 %all-to-all-start = ((bf16[32,8,128]{2,1,0:T(8,128)(2,1)}), bf16[32,8,128]{2,1,0:T(8,128)(2,1)S(1)}, u32[]{:S(2)}, u32[]{:S(2)}) async-start(bf16[32,8,128]{2,1,0:T(8,128)(2,1)} %broadcast_in_dim.8), calls=%async_computation | async-start | bytes 131072 | tf_op jit(solution)/shard_map/all_to_all | solution.py:135
  22.0 0.6 copy-start

commit v2 on v1

v2 whole, which is shorter than its diff:
```python
import math

import jax
import jax.numpy as jnp
from jax import lax
from jax.experimental import pallas as pl
from jax.experimental.pallas import tpu as pltpu
from jax.sharding import PartitionSpec as P

QUERY_HEADS = 64
KEY_VALUE_HEADS = 8
HEAD_SIZE = 128
BLOCK = 512
GROUP = QUERY_HEADS // KEY_VALUE_HEADS
SCALE = 1.0 / math.sqrt(HEAD_SIZE)
LOW = -1e30
LIVE_BITS = 10

VMEM = pl.BlockSpec(memory_space=pltpu.VMEM)
SMEM = pl.BlockSpec(memory_space=pltpu.SMEM)
ANY = pl.BlockSpec(memory_space=pl.ANY)
PIECES = 2


def load(*copies):
    for copy in copies:
        copy.start()
    for copy in copies:
        copy.wait()


def spread_kernel(query_hbm, key_hbm, value_hbm, out_ref, own_ref, query, key, value, sems):
    pairs = ((query_hbm, query), (key_hbm, key), (value_hbm, value))
    load(*(pltpu.make_async_copy(*pair, sems.at[i]) for i, pair in enumerate(pairs)))
    wide = query[...].astype(jnp.float32)
    heads = [wide[:, head * HEAD_SIZE : (head + 1) * HEAD_SIZE] for head in range(GROUP)]
    heads = jnp.concatenate(heads, axis=0)
    out_ref[...] = jnp.broadcast_to(heads.astype(jnp.bfloat16)[None], out_ref.shape)
    score = SCALE * jnp.sum(heads * key[...].astype(jnp.float32), axis=-1, keepdims=True)
    own_ref[0] = jnp.broadcast_to(score, (GROUP, HEAD_SIZE))
    own_ref[1] = jnp.broadcast_to(value[...].astype(jnp.float32), (GROUP, HEAD_SIZE))


def slots_kernel(device_ref, lengths_hbm, placement_hbm, code_ref, lengths, placement, sems):
    pairs = ((lengths_hbm, lengths), (placement_hbm, placement))
    load(*(pltpu.make_async_copy(*pair, sems.at[i]) for i, pair in enumerate(pairs)))
    slots = code_ref.shape[0]
    places = placement[...] - device_ref[0] * slots
    row = lax.broadcasted_iota(jnp.int32, places.shape, 0)
    length = jnp.zeros_like(places)
    for r in range(lengths_hbm.shape[0]):
        length = jnp.where(row == r, lengths[r], length)
    start = lax.broadcasted_iota(jnp.int32, places.shape, 1) * BLOCK
    code = (row << LIVE_BITS) + jnp.clip(length - start, 0, BLOCK)
    for slot in range(slots):
        code_ref[slot] = jnp.sum(jnp.where(places == slot, code, 0))


def attention_kernel(
    device_ref,
    code_ref,
    query_ref,
    own_ref,
    key_hbm,
    value_hbm,
    out_ref,
    keys,
    values,
    sems,
    scores,
    peaks,
    masses,
    sums,
):
    slots, block, _ = keys.shape
    rows = query_ref.shape[0]
    device = device_ref[0]
    per_piece = slots // PIECES
    copies = [
        [
            pltpu.make_async_copy(
                source.at[pl.ds(piece * per_piece, per_piece)],
                target.at[pl.ds(piece * per_piece, per_piece)],
                sems.at[which, piece],
            )
            for piece in range(PIECES)
        ]
        for which, (source, target) in enumerate(((key_hbm, keys), (value_hbm, values)))
    ]
    for copy in (*copies[0], *copies[1]):
        copy.start()

    contract_last = (((1,), (1,)), ((), ()))
    position = lax.broadcasted_iota(jnp.int32, (GROUP, block), 1)
    lane = lax.broadcasted_iota(jnp.int32, (rows, GROUP, 128), 2)
    masses[...] = jnp.zeros_like(masses)
    sums[...] = jnp.zeros_like(sums)
    peaks[...] = jnp.full_like(peaks, LOW)
    own_score = own_ref[0]
    peaks[device] = own_score

    held = []
    for slot in range(slots):
        code = code_ref[slot]
        held.append((code >> LIVE_BITS, code & ((1 << LIVE_BITS) - 1)))
    for slot, (row, live) in enumerate(held):
        if slot % per_piece == 0:
            copies[0][slot // per_piece].wait()
        s = lax.dot_general(
            query_ref[row], keys[slot], contract_last, preferred_element_type=jnp.float32
        )
        s = jnp.where(position < live, s * SCALE, LOW)
        scores[slot] = s
        top = s[:, :128]
        for part in range(1, block // 128):
            top = jnp.maximum(top, s[:, part * 128 : (part + 1) * 128])
        peaks[row] = jnp.maximum(peaks[row], top)
    top = jnp.max(peaks[...], axis=-1, keepdims=True)
    top = top.astype(jnp.bfloat16).astype(jnp.float32)
    peaks[...] = jnp.broadcast_to(top, peaks.shape)
    own_weight = jnp.exp(own_score - peaks[device])
    masses[device] = jnp.where(lane[0] == 0, own_weight, 0.0)
    sums[device] = own_weight.astype(jnp.bfloat16).astype(jnp.float32) * own_ref[1]
    for slot, (row, live) in enumerate(held):
        if slot % per_piece == 0:
            copies[1][slot // per_piece].wait()
        w = jnp.exp(scores[slot] - jnp.tile(peaks[row], (1, block // 128)))
        w = jnp.where(position < live, w, 0.0)
        mass = w[:, :128]
        for part in range(1, block // 128):
            mass = mass + w[:, part * 128 : (part + 1) * 128]
        masses[row] = masses[row] + mass
        sums[row] = sums[row] + jnp.dot(
            w.astype(jnp.bfloat16), values[slot], preferred_element_type=jnp.float32
        )
    mass = jnp.sum(masses[...], axis=-1, keepdims=True)
    high = mass.astype(jnp.bfloat16).astype(jnp.float32)
    extra = jnp.where(lane == 0, peaks[...], jnp.where(lane == 1, high, mass - high))
    out_ref[...] = jnp.concatenate([sums[...], extra], axis=1).astype(jnp.bfloat16)


def finish_kernel(parts_ref, out_ref):
    parts = parts_ref[...].astype(jnp.float32)
    partial = parts[:, :GROUP]
    extra = parts[:, GROUP:]
    peaks = extra[:, :, 0:1]
    highest = jnp.max(peaks, axis=0, keepdims=True)
    factor = jnp.exp(peaks - highest)
    masses = extra[:, :, 1:2] + extra[:, :, 2:3]
    denominator = jnp.sum(masses * factor, axis=0)
    total = jnp.sum(partial * factor, axis=0)
    attended = (total / denominator).astype(jnp.bfloat16)
    out_ref[...] = jnp.broadcast_to(attended[None], out_ref.shape)


def project_kernel(attended_ref, w_ref, out_ref):
    heads = jnp.swapaxes(attended_ref[...].astype(jnp.float32), 0, 1).astype(jnp.bfloat16)
    total = None
    for head in range(GROUP):
        term = jnp.dot(
            heads[head],
            w_ref[head * HEAD_SIZE : (head + 1) * HEAD_SIZE, :],
            preferred_element_type=jnp.float32,
        )
        total = term if total is None else total + term
    ranks, packed, full = out_ref.shape
    width = total.shape[1] // ranks
    for rank in range(ranks):
        block = total[:, rank * width : (rank + 1) * width]
        out_ref[rank] = jnp.concatenate(
            [block[i * packed : (i + 1) * packed] for i in range(full // width)], axis=1
        )


def sum_kernel(terms_ref, out_ref):
    total = jnp.sum(terms_ref[...], axis=0)
    width = out_ref.shape[1]
    out_ref[...] = jnp.concatenate(
        [total[:, i * width : (i + 1) * width] for i in range(total.shape[1] // width)], axis=0
    ).astype(jnp.bfloat16)


def in_hbm(x):
    return pltpu.with_memory_space_constraint(x, pltpu.HBM)


def call(kernel, name, out_shape, in_specs, scratch_shapes=(), megabytes=2):
    return pl.pallas_call(
        kernel,
        out_shape=out_shape,
        in_specs=in_specs,
        out_specs=jax.tree.map(lambda _: VMEM, out_shape),
        scratch_shapes=scratch_shapes,
        compiler_params=pltpu.CompilerParams(vmem_limit_bytes=megabytes << 20),
        name=name,
    )


def shards(
    queries,
    fresh_keys,
    fresh_values,
    key_cache_blocks,
    value_cache_blocks,
    lengths,
    placement,
    w_out,
):
    rows = lengths.shape[0]
    slots, block, _ = key_cache_blocks.shape
    device = lax.axis_index("attn").astype(jnp.int32).reshape(1)
    ranks = lax.axis_size("tensor")
    per_row = jax.ShapeDtypeStruct((rows, GROUP, HEAD_SIZE), jnp.bfloat16)

    fresh = (queries, fresh_keys, fresh_values)
    spread, own = call(
        spread_kernel,
        "spread",
        (per_row, jax.ShapeDtypeStruct((2, GROUP, HEAD_SIZE), jnp.float32)),
        [ANY] * 3,
        [pltpu.VMEM(a.shape, a.dtype) for a in fresh] + [pltpu.SemaphoreType.DMA((3,))],
    )(*map(in_hbm, fresh))
    every_query = lax.all_to_all(spread, "attn", 0, 0, tiled=True)
    codes = pl.pallas_call(
        slots_kernel,
        out_shape=jax.ShapeDtypeStruct((slots,), jnp.int32),
        in_specs=[SMEM, ANY, ANY],
        out_specs=SMEM,
        scratch_shapes=[
            pltpu.SMEM(lengths.shape, jnp.int32),
            pltpu.VMEM(placement.shape, jnp.int32),
            pltpu.SemaphoreType.DMA((2,)),
        ],
        compiler_params=pltpu.CompilerParams(vmem_limit_bytes=2 << 20),
        name="slots",
    )(device, in_hbm(lengths), in_hbm(placement))
    cache = pltpu.VMEM(key_cache_blocks.shape, jnp.bfloat16)
    state = pltpu.VMEM((rows, GROUP, 128), jnp.float32)
    partials = call(
        attention_kernel,
        "attention",
        jax.ShapeDtypeStruct((rows, 2 * GROUP, HEAD_SIZE), jnp.bfloat16),
        [SMEM, SMEM, VMEM, VMEM, ANY, ANY],
        [
            cache,
            cache,
            pltpu.SemaphoreType.DMA((2, PIECES)),
            pltpu.VMEM((slots, GROUP, block), jnp.float32),
            state,
            state,
            state,
        ],
        16,
    )(
        device,
        codes,
        every_query,
        own,
        in_hbm(key_cache_blocks),
        in_hbm(value_cache_blocks),
    )
    partials = lax.all_to_all(partials, "attn", 0, 0, tiled=True)
    attended = call(finish_kernel, "finish", per_row, [VMEM])(partials)
    attended = lax.all_to_all(attended, "attn", 0, 0, tiled=True)

    width = w_out.shape[1] // ranks
    terms = call(
        project_kernel,
        "project",
        jax.ShapeDtypeStruct((ranks, rows * width // 128, 128), jnp.float32),
        [VMEM, VMEM],
        (),
        4,
    )(attended, w_out)
    terms = lax.all_to_all(terms, "tensor", 0, 0, tiled=True)
    return call(sum_kernel, "sum", jax.ShapeDtypeStruct((rows, width), jnp.bfloat16), [VMEM])(terms)


def solution(mesh):
    return jax.shard_map(
        shards,
        mesh=mesh,
        in_specs=(
            P("attn", "tensor"),
            P("attn", "tensor"),
            P("attn", "tensor"),
            P("attn", None, "tensor"),
            P("attn", None, "tensor"),
            P(),
            P(),
            P("tensor", "attn"),
        ),
        out_specs=P(None, ("attn", "tensor")),
        check_vma=False,
    )
```

time: 76.9 us -> 66 us (0.86)
  local copies, waits for them, and re-layouts: 4.21 us -> 0.01 us
  Pallas kernels: 11.6 us -> 8.63 us
  blocking collectives: 40.8 us -> 37.9 us
  other arithmetic: 2.04 us -> 0 us
  waiting for transfers between devices: 5.82 us -> 7.13 us
    pallas_call x3 -> x5, Pallas kernels: 9.96 us -> 6.96 us  [the longest x1 4.45 us: shards(): call(attention_kernel, 'attention', jax.ShapeDtypeStruct((rows, 2 * GROUP...]
    unnamed x6 -> x2, local copies, waits for them, and re-layouts: 1.73 us -> 0.01 us
    all_to_all x1, blocking collectives: 13.9 us -> 12.5 us  [shards(): partials = lax.all_to_all(partials, 'attn', 0, 0, tiled=True)]
    reshape x1 -> x0, local copies, waits for them, and re-layouts: 1.34 us -> none  [shards(): lengths.reshape(rows, 1)]
    all_to_all x1, waiting for transfers between devices: 5.82 us -> 7.13 us  [shards(): every_query = lax.all_to_all(spread, 'attn', 0, 0, tiled=True)]
    all_to_all x1, blocking collectives: 13.4 us -> 12.1 us  [shards(): attended = lax.all_to_all(attended, 'attn', 0, 0, tiled=True)]
  transfers between devices with their start and end apart: 1 -> 1, of which waited for: 1 -> 1; matrix products, arithmetic and copies ran while one was open for 2% -> 0% of each run, Pallas kernels for 2% -> 3%
where the time goes in v2:
time: 66 us; the launch traced here: 65.6 us
  blocking collectives  37.9 us (57%)
  starting transfers between devices  11.9 us (18%)
  Pallas kernels  8.63 us (13%)
  waiting for transfers between devices  7.13 us (11%)
    all_to_all x1, blocking collectives, shards(): terms = lax.all_to_all(terms, 'tensor', 0, 0, tiled=True)  13.4 us
    all_to_all x1, blocking collectives, shards(): partials = lax.all_to_all(partials, 'attn', 0, 0, tiled=True)  12.5 us
    all_to_all x1, blocking collectives, shards(): attended = lax.all_to_all(attended, 'attn', 0, 0, tiled=True)  12.1 us
    all_to_all x1, starting transfers between devices, shards(): every_query = lax.all_to_all(spread, 'attn', 0, 0, tiled=True)  11.9 us
    all_to_all x1, waiting for transfers between devices, shards(): every_query = lax.all_to_all(spread, 'attn', 0, 0, tiled=True)  7.13 us
    pallas_call x1, Pallas kernels, shards(): call(attention_kernel, 'attention', jax.ShapeDtypeStruct((rows, 2 * GROUP...  4.45 us
    pallas_call x1, Pallas kernels, shards(): pl.pallas_call(slots_kernel, out_shape=jax.ShapeDtypeStruct((slots,), jnp...  1.68 us
    pallas_call x1, Pallas kernels, shards(): call(spread_kernel, 'spread', (per_row, jax.ShapeDtypeStruct((2, GROUP, H...  1.34 us
  transfers between devices with their start and end apart: 1, of which 1 were waited for; matrix products, arithmetic and copies ran while one was open for 0% of the time, Pallas kernels for 3%

profile of v2, /device:TPU:1, one launch (start us, length us, event | category | flops | bytes accessed | tf_op | source)
XLA Modules:
  0.0 65.6 jit_solution(14679312548104426074)
XLA Ops:
  0.0 1.3 %spread.1 = (bf16[32,8,128]{2,1,0:T(8,128)(2,1)}, f32[2,8,128]{2,1,0:T(8,128)S(1)}) custom-call(bf16[1,1024]{1,0:T(2,128)(2,1)} %query_hbm.1, bf16[1,128]{1,0:T(2,128)(2,1)} %key_hbm.2, bf16[1,128]{1,0:T(2,128)(2,1)} %value_hbm.2), custom_call_target="tpu_custom_call" | custom-call | tf_op jit(solution)/shard_map/spread/pallas_call | solution.py:216
  1.4 11.9 %all-to-all-start = ((bf16[32,8,128]{2,1,0:T(8,128)(2,1)}), bf16[32,8,128]{2,1,0:T(8,128)(2,1)S(1)}, u32[]{:S(2)}, u32[]{:S(2)}) async-start(bf16[32,8,128]{2,1,0:T(8,128)(2,1)} %get-tuple-element.7), calls=%async_computation | async-start | bytes 131072 | tf_op jit(solution)/shard_map/all_to_all | solution.py:223
  13.2 1.7 %slots.1.code_ref = s32[32]{0:T(128)S(1)} custom-call(s32[1]{0:T(128)} %bitcast.device_ref, s32[32]{0:T(128)} %lengths_hbm.1, s32[32,249]{1,0:T(8,128)} %placement_hbm.1), custom_call_target="tpu_custom_call" | custom-call | tf_op jit(solution)/shard_map/slots/pallas_call | solution.py:224
  14.9 7.1 %all-to-all-done.query_ref = bf16[32,8,128]{2,1,0:T(8,128)(2,1)S(1)} async-done(((bf16[32,8,128]{2,1,0:T(8,128)(2,1)}), bf16[32,8,128]{2,1,0:T(8,128)(2,1)S(1)}, u32[]{:S(2)}, u32[]{:S(2)}) %all-to-all-start) | async-done | bytes 65568 | tf_op jit(solution)/shard_map/all_to_all | solution.py:223
  22.1 0.0 copy-start
  22.1 4.5 %attention.1 = bf16[32,16,128]{2,1,0:T(8,128)(2,1)S(1)} custom-call(s32[1]{0:T(128)} %bitcast.device_ref, s32[32]{0:T(128)S(1)} %slots.1.code_ref, bf16[32,8,128]{2,1,0:T(8,128)(2,1)S(1)} %all-to-all-done.query_ref, f32[2,8,128]{2,1,0:T(8,128)S(1)} %get-tuple-element.8.own_ref, bf16[32,512,128]{2,1,0:T(8,128)(2,1)} %key_hbm.3, bf16[32,512,128]{2,1,0:T(8,128)(2,1)} %value_hbm.3), custom_call_target="tpu_custom_call" | custom-call | tf_op jit(solution)/shard_map/attention/pallas_call | solution.py:239
  26.5 12.5 %all_to_all.20.parts_ref = bf16[32,16,128]{2,1,0:T(8,128)(2,1)S(1)} all-to-all(bf16[32,16,128]{2,1,0:T(8,128)(2,1)S(1)} %attention.1), channel_id=1, replica_groups=mesh['attn'=32,'tensor'=8] {'attn'}, dimensions={0} | all-to-all | bytes 262144 | tf_op jit(solution)/shard_map/all_to_all | solution.py:262
  39.0 0.2 finish.1
  39.2 12.1 %all_to_all.21.attended_ref = bf16[32,8,128]{2,1,0:T(8,128)(2,1)S(1)} all-to-all(bf16[32,8,128]{2,1,0:T(8,128)(2,1)S(1)} %finish.1), channel_id=1, replica_groups=mesh['attn'=32,'tensor'=8] {'attn'}, dimensions={0} | all-to-all | bytes 131072 | tf_op jit(solution)/shard_map/all_to_all | solution.py:264
  51.3 0.0 copy-done
  51.3 0.3 project.1
  51.6 13.4 %all_to_all.22.terms_ref = f32[8,8,128]{2,1,0:T(8,128)S(1)} all-to-all(f32[8,8,128]{2,1,0:T(8,128)S(1)} %project.1), channel_id=1, replica_groups=mesh['attn'=32,'tensor'=8] {'tensor'}, dimensions={0} | all-to-all | bytes 65536 | tf_op jit(solution)/shard_map/all_to_all | solution.py:275
  65.0 0.7 %sum.1 = bf16[32,32]{1,0:T(8,128)(2,1)} custom-call(f32[8,8,128]{2,1,0:T(8,128)S(1)} %all_to_all.22.terms_ref), custom_call_target="tpu_custom_call" | custom-call | tf_op jit(solution)/shard_map/sum/pallas_call | solution.py:276
Async XLA Ops:
  1.4 20.7 %all-to-all-start = ((bf16[32,8,128]{2,1,0:T(8,128)(2,1)}), bf16[32,8,128]{2,1,0:T(8,128)(2,1)S(1)}, u32[]{:S(2)}, u32[]{:S(2)}) async-start(bf16[32,8,128]{2,1,0:T(8,128)(2,1)} %get-tuple-element.7), calls=%async_computation | async-start | bytes 131072 | tf_op jit(solution)/shard_map/all_to_all | solution.py:223
  22.1 29.3 %copy-start = (bf16[1024,256]{1,0:T(8,128)(2,1)S(1)}, bf16[1024,256]{1,0:T(8,128)(2,1)}, u32[]{:S(2)}) copy-start(bf16[1024,256]{1,0:T(8,128)(2,1)} %w_ref.1) | copy-start | bytes 1572868

commit v3 on v2

v3 whole, which is shorter than its diff:
```python
import math

import jax
import jax.numpy as jnp
from jax import lax
from jax.experimental import pallas as pl
from jax.experimental.pallas import tpu as pltpu
from jax.sharding import PartitionSpec as P

QUERY_HEADS = 64
KEY_VALUE_HEADS = 8
HEAD_SIZE = 128
BLOCK = 512
GROUP = QUERY_HEADS // KEY_VALUE_HEADS
SCALE = 1.0 / math.sqrt(HEAD_SIZE)
LOW = -(2.0**99)
LIVE_BITS = 10

VMEM = pl.BlockSpec(memory_space=pltpu.VMEM)
SMEM = pl.BlockSpec(memory_space=pltpu.SMEM)
ANY = pl.BlockSpec(memory_space=pl.ANY)


def spread_kernel(
    query_hbm,
    key_hbm,
    value_hbm,
    lengths_hbm,
    placement_hbm,
    key_cache_hbm,
    value_cache_hbm,
    out_ref,
    own_ref,
    code_ref,
    query,
    key,
    value,
    lengths,
    placement,
    sems,
):
    pairs = (
        (query_hbm, query),
        (key_hbm, key),
        (value_hbm, value),
        (lengths_hbm, lengths),
        (placement_hbm, placement),
    )
    copies = [pltpu.make_async_copy(*pair, sems.at[i]) for i, pair in enumerate(pairs)]
    for copy in copies:
        copy.start()
    for copy in copies:
        copy.wait()
    wide = query[...].astype(jnp.float32)
    heads = [wide[:, head * HEAD_SIZE : (head + 1) * HEAD_SIZE] for head in range(GROUP)]
    heads = jnp.concatenate(heads, axis=0)
    out_ref[...] = jnp.broadcast_to(heads.astype(jnp.bfloat16)[None], out_ref.shape)
    score = SCALE * jnp.sum(heads * key[...].astype(jnp.float32), axis=-1, keepdims=True)
    device = lax.axis_index("attn")
    own = lax.broadcasted_iota(jnp.int32, out_ref.shape, 0) == device
    own_ref[0] = jnp.where(own, score[None], LOW)
    own_ref[1] = jnp.where(own, value[...].astype(jnp.float32)[None], 0.0)

    slots = code_ref.shape[0]
    places = placement[...] - device * slots
    row = lax.broadcasted_iota(jnp.int32, places.shape, 0)
    length = jnp.zeros_like(places)
    for r in range(lengths.shape[0]):
        length = jnp.where(row == r, lengths[r], length)
    start = lax.broadcasted_iota(jnp.int32, places.shape, 1) * BLOCK
    code = (row << LIVE_BITS) + jnp.clip(length - start, 0, BLOCK)
    for slot in range(slots):
        code_ref[slot] = jnp.sum(jnp.where(places == slot, code, 0))


def attention_kernel(
    code_ref,
    query_ref,
    own_ref,
    key_ref,
    value_ref,
    out_ref,
    scores,
    peaks,
    masses,
    sums,
):
    slots, block, _ = key_ref.shape
    rows = query_ref.shape[0]
    contract_last = (((1,), (1,)), ((), ()))
    position = lax.broadcasted_iota(jnp.int32, (GROUP, block), 1)
    lane = lax.broadcasted_iota(jnp.int32, (rows, GROUP, 128), 2)
    peaks[...] = own_ref[0]
    held = []
    for slot in range(slots):
        code = code_ref[slot]
        held.append((code >> LIVE_BITS, code & ((1 << LIVE_BITS) - 1)))
    for slot, (row, live) in enumerate(held):
        s = lax.dot_general(
            query_ref[row], key_ref[slot], contract_last, preferred_element_type=jnp.float32
        )
        s = jnp.where(position < live, s * SCALE, LOW)
        scores[slot] = s
        top = s[:, :128]
        for part in range(1, block // 128):
            top = jnp.maximum(top, s[:, part * 128 : (part + 1) * 128])
        peaks[row] = jnp.maximum(peaks[row], top)
    top = jnp.max(peaks[...], axis=-1, keepdims=True)
    top = top.astype(jnp.bfloat16).astype(jnp.float32)
    peaks[...] = jnp.broadcast_to(top, peaks.shape)
    own_weight = jnp.exp(own_ref[0] - peaks[...])
    masses[...] = jnp.where(lane == 0, own_weight, 0.0)
    sums[...] = own_weight.astype(jnp.bfloat16).astype(jnp.float32) * own_ref[1]
    for slot, (row, live) in enumerate(held):
        w = jnp.exp(scores[slot] - jnp.tile(peaks[row], (1, block // 128)))
        w = jnp.where(position < live, w, 0.0)
        mass = w[:, :128]
        for part in range(1, block // 128):
            mass = mass + w[:, part * 128 : (part + 1) * 128]
        masses[row] = masses[row] + mass
        sums[row] = sums[row] + jnp.dot(
            w.astype(jnp.bfloat16), value_ref[slot], preferred_element_type=jnp.float32
        )
    mass = jnp.sum(masses[...], axis=-1, keepdims=True)
    high = mass.astype(jnp.bfloat16).astype(jnp.float32)
    extra = jnp.where(lane == 0, peaks[...], jnp.where(lane == 1, high, mass - high))
    out_ref[...] = jnp.concatenate([sums[...], extra], axis=1).astype(jnp.bfloat16)


def finish_kernel(parts_ref, out_ref):
    parts = parts_ref[...].astype(jnp.float32)
    partial = parts[:, :GROUP]
    extra = parts[:, GROUP:]
    peaks = extra[:, :, 0:1]
    highest = jnp.max(peaks, axis=0, keepdims=True)
    factor = jnp.exp(peaks - highest)
    masses = extra[:, :, 1:2] + extra[:, :, 2:3]
    denominator = jnp.sum(masses * factor, axis=0)
    total = jnp.sum(partial * factor, axis=0)
    attended = (total / denominator).astype(jnp.bfloat16)
    out_ref[...] = jnp.broadcast_to(attended[None], out_ref.shape)


def project_kernel(attended_ref, w_ref, out_ref):
    heads = jnp.swapaxes(attended_ref[...].astype(jnp.float32), 0, 1).astype(jnp.bfloat16)
    total = None
    for head in range(GROUP):
        term = jnp.dot(
            heads[head],
            w_ref[head * HEAD_SIZE : (head + 1) * HEAD_SIZE, :],
            preferred_element_type=jnp.float32,
        )
        total = term if total is None else total + term
    ranks, packed, full = out_ref.shape
    width = total.shape[1] // ranks
    for rank in range(ranks):
        block = total[:, rank * width : (rank + 1) * width]
        out_ref[rank] = jnp.concatenate(
            [block[i * packed : (i + 1) * packed] for i in range(full // width)], axis=1
        )


def sum_kernel(terms_ref, out_ref):
    total = jnp.sum(terms_ref[...], axis=0)
    width = out_ref.shape[1]
    out_ref[...] = jnp.concatenate(
        [total[:, i * width : (i + 1) * width] for i in range(total.shape[1] // width)], axis=0
    ).astype(jnp.bfloat16)


def in_hbm(x):
    return pltpu.with_memory_space_constraint(x, pltpu.HBM)


def call(kernel, name, out_shape, in_specs, scratch_shapes=(), megabytes=2):
    return pl.pallas_call(
        kernel,
        out_shape=out_shape,
        in_specs=in_specs,
        out_specs=jax.tree.map(lambda _: VMEM, out_shape),
        scratch_shapes=scratch_shapes,
        compiler_params=pltpu.CompilerParams(vmem_limit_bytes=megabytes << 20),
        name=name,
    )


def shards(
    queries,
    fresh_keys,
    fresh_values,
    key_cache_blocks,
    value_cache_blocks,
    lengths,
    placement,
    w_out,
):
    rows = lengths.shape[0]
    slots, block, _ = key_cache_blocks.shape
    ranks = lax.axis_size("tensor")
    per_row = jax.ShapeDtypeStruct((rows, GROUP, HEAD_SIZE), jnp.bfloat16)

    small = (queries, fresh_keys, fresh_values, lengths, placement)
    room = [pltpu.VMEM(a.shape, a.dtype) for a in small]
    room[3] = pltpu.SMEM(lengths.shape, jnp.int32)
    spread, own, codes = pl.pallas_call(
        spread_kernel,
        out_shape=(
            per_row,
            jax.ShapeDtypeStruct((2, *per_row.shape), jnp.float32),
            pltpu.SMEM((slots,), jnp.int32),
        ),
        in_specs=[ANY] * (len(small) + 2),
        out_specs=(VMEM, VMEM, SMEM),
        scratch_shapes=room + [pltpu.SemaphoreType.DMA((len(small),))],
        compiler_params=pltpu.CompilerParams(vmem_limit_bytes=2 << 20),
        cost_estimate=pl.CostEstimate(
            flops=1 << 30, bytes_accessed=64 << 20, transcendentals=0
        ),
        name="spread",
    )(*map(in_hbm, (*small, key_cache_blocks, value_cache_blocks)))
    every_query = lax.all_to_all(spread, "attn", 0, 0, tiled=True)
    state = pltpu.VMEM((rows, GROUP, 128), jnp.float32)
    partials = call(
        attention_kernel,
        "attention",
        jax.ShapeDtypeStruct((rows, 2 * GROUP, HEAD_SIZE), jnp.bfloat16),
        [SMEM, VMEM, VMEM, VMEM, VMEM],
        [pltpu.VMEM((slots, GROUP, block), jnp.float32), state, state, state],
        4,
    )(codes, every_query, own, key_cache_blocks, value_cache_blocks)
    partials = lax.all_to_all(partials, "attn", 0, 0, tiled=True)
    attended = call(finish_kernel, "finish", per_row, [VMEM])(partials)
    attended = lax.all_to_all(attended, "attn", 0, 0, tiled=True)

    width = w_out.shape[1] // ranks
    terms = call(
        project_kernel,
        "project",
        jax.ShapeDtypeStruct((ranks, rows * width // 128, 128), jnp.float32),
        [VMEM, VMEM],
        (),
        4,
    )(attended, w_out)
    terms = lax.all_to_all(terms, "tensor", 0, 0, tiled=True)
    return call(sum_kernel, "sum", jax.ShapeDtypeStruct((rows, width), jnp.bfloat16), [VMEM])(terms)


def solution(mesh):
    return jax.shard_map(
        shards,
        mesh=mesh,
        in_specs=(
            P("attn", "tensor"),
            P("attn", "tensor"),
            P("attn", "tensor"),
            P("attn", None, "tensor"),
            P("attn", None, "tensor"),
            P(),
            P(),
            P("tensor", "attn"),
        ),
        out_specs=P(None, ("attn", "tensor")),
        check_vma=False,
    )
```

time: 66 us -> 63.5 us (0.962)
  blocking collectives: 37.9 us -> 58.7 us
  starting transfers between devices: 11.9 us -> 0 us
  waiting for transfers between devices: 7.13 us -> 0 us
  Pallas kernels: 8.63 us -> 4.53 us
    all_to_all x0 -> x1, blocking collectives: none -> 20.7 us  [shards(): every_query = lax.all_to_all(spread, 'attn', 0, 0, tiled=True)]
    all_to_all x1 -> x0, starting transfers between devices: 11.9 us -> none  [shards(): every_query = lax.all_to_all(spread, 'attn', 0, 0, tiled=True)]
    all_to_all x1 -> x0, waiting for transfers between devices: 7.13 us -> none  [shards(): every_query = lax.all_to_all(spread, 'attn', 0, 0, tiled=True)]
    pallas_call x1, Pallas kernels: 4.45 us -> 2.06 us  [shards(): call(attention_kernel, 'attention', jax.ShapeDtypeStruct((rows, 2 * GROUP...]
    pallas_call x2 -> x1, Pallas kernels: 3.02 us -> 1.31 us  [shards(): pl.pallas_call(spread_kernel, out_shape=(per_row, jax.ShapeDtypeStruct((2...]
  transfers between devices with their start and end apart: 1 -> 0, of which waited for: 1 -> 0; matrix products, arithmetic and copies ran while one was open for 0% -> 0% of each run, Pallas kernels for 3% -> 0%
where the time goes in v3:
time: 63.5 us; the launch traced here: 63.3 us
  blocking collectives  58.7 us (92%)
  Pallas kernels  4.53 us (7%)
    all_to_all x1, blocking collectives, shards(): every_query = lax.all_to_all(spread, 'attn', 0, 0, tiled=True)  20.7 us
    all_to_all x1, blocking collectives, shards(): terms = lax.all_to_all(terms, 'tensor', 0, 0, tiled=True)  13.4 us
    all_to_all x1, blocking collectives, shards(): partials = lax.all_to_all(partials, 'attn', 0, 0, tiled=True)  12.5 us
    all_to_all x1, blocking collectives, shards(): attended = lax.all_to_all(attended, 'attn', 0, 0, tiled=True)  12.1 us
    pallas_call x1, Pallas kernels, shards(): call(attention_kernel, 'attention', jax.ShapeDtypeStruct((rows, 2 * GROUP...  2.06 us
    pallas_call x1, Pallas kernels, shards(): pl.pallas_call(spread_kernel, out_shape=(per_row, jax.ShapeDtypeStruct((2...  1.31 us

profile of v3, /device:TPU:1, one launch (start us, length us, event | category | flops | bytes accessed | tf_op | source)
XLA Modules:
  0.0 63.3 jit_solution(8851295698608398757)
XLA Ops:
  0.0 0.0 copy-start.1
  0.0 0.0 copy-start
  0.0 1.3 %spread.1 = (bf16[32,8,128]{2,1,0:T(8,128)(2,1)S(1)}, f32[2,32,8,128]{3,2,1,0:T(8,128)S(1)}, s32[32]{0:T(128)S(4)}) custom-call(bf16[1,1024]{1,0:T(2,128)(2,1)} %query_hbm.1, bf16[1,128]{1,0:T(2,128)(2,1)} %key_hbm.1, bf16[1,128]{1,0:T(2,128)(2,1)} %value_hbm.1, s32[32]{0:T(128)} %lengths_hbm.1, s32[32,249]{1,0:T(8,128)} %placement_hbm.1, ...), custom_call_target="tpu_custom_call" | custom-call | flops 1073741824 | bytes 67108864 | tf_op jit(solution)/shard_map/spread/pallas_call | solution.py:205
  1.3 20.7 %all_to_all.20.query_ref = bf16[32,8,128]{2,1,0:T(8,128)(2,1)S(1)} all-to-all(bf16[32,8,128]{2,1,0:T(8,128)(2,1)S(1)} %get-tuple-element.9), channel_id=1, replica_groups=mesh['attn'=32,'tensor'=8] {'attn'}, dimensions={0} | all-to-all | bytes 131072 | tf_op jit(solution)/shard_map/all_to_all | solution.py:221
  22.1 0.0 copy-done.1
  22.1 0.0 copy-done
  22.1 0.0 copy-start.2
  22.1 2.1 %attention.1 = bf16[32,16,128]{2,1,0:T(8,128)(2,1)S(1)} custom-call(s32[32]{0:T(128)S(4)} %get-tuple-element.8.code_ref, bf16[32,8,128]{2,1,0:T(8,128)(2,1)S(1)} %all_to_all.20.query_ref, f32[2,32,8,128]{3,2,1,0:T(8,128)S(1)} %get-tuple-element.10.own_ref, bf16[32,512,128]{2,1,0:T(8,128)(2,1)S(1)} %copy-done, bf16[32,512,128]{2,1,0:T(8,128)(2,1)S(1)} %copy-done.1), custom_call_target="tpu_custom_call" | custom-call | tf_op jit(solution)/shard_map/attention/pallas_call | solution.py:223
  24.1 12.5 %all_to_all.21.parts_ref = bf16[32,16,128]{2,1,0:T(8,128)(2,1)S(1)} all-to-all(bf16[32,16,128]{2,1,0:T(8,128)(2,1)S(1)} %attention.1), channel_id=1, replica_groups=mesh['attn'=32,'tensor'=8] {'attn'}, dimensions={0} | all-to-all | bytes 262144 | tf_op jit(solution)/shard_map/all_to_all | solution.py:231
  36.6 0.2 finish.1
  36.8 12.1 %all_to_all.22.attended_ref = bf16[32,8,128]{2,1,0:T(8,128)(2,1)S(1)} all-to-all(bf16[32,8,128]{2,1,0:T(8,128)(2,1)S(1)} %finish.1), channel_id=1, replica_groups=mesh['attn'=32,'tensor'=8] {'attn'}, dimensions={0} | all-to-all | bytes 131072 | tf_op jit(solution)/shard_map/all_to_all | solution.py:233
  49.0 0.0 copy-done.2
  49.0 0.3 project.1
  49.2 13.4 %all_to_all.23.terms_ref = f32[8,8,128]{2,1,0:T(8,128)S(1)} all-to-all(f32[8,8,128]{2,1,0:T(8,128)S(1)} %project.1), channel_id=1, replica_groups=mesh['attn'=32,'tensor'=8] {'tensor'}, dimensions={0} | all-to-all | bytes 65536 | tf_op jit(solution)/shard_map/all_to_all | solution.py:244
  62.6 0.7 %sum.1 = bf16[32,32]{1,0:T(8,128)(2,1)} custom-call(f32[8,8,128]{2,1,0:T(8,128)S(1)} %all_to_all.23.terms_ref), custom_call_target="tpu_custom_call" | custom-call | tf_op jit(solution)/shard_map/sum/pallas_call | solution.py:245
Async XLA Ops:
  0.0 22.1 %copy-start.1 = (bf16[32,512,128]{2,1,0:T(8,128)(2,1)S(1)}, bf16[32,512,128]{2,1,0:T(8,128)(2,1)}, u32[]{:S(2)}) copy-start(bf16[32,512,128]{2,1,0:T(8,128)(2,1)} %value_ref.1) | copy-start | bytes 12582916
  0.0 22.1 %copy-start = (bf16[32,512,128]{2,1,0:T(8,128)(2,1)S(1)}, bf16[32,512,128]{2,1,0:T(8,128)(2,1)}, u32[]{:S(2)}) copy-start(bf16[32,512,128]{2,1,0:T(8,128)(2,1)} %key_ref.1) | copy-start | bytes 12582916
  22.1 26.9 %copy-start.2 = (bf16[1024,256]{1,0:T(8,128)(2,1)S(1)}, bf16[1024,256]{1,0:T(8,128)(2,1)}, u32[]{:S(2)}) copy-start(bf16[1024,256]{1,0:T(8,128)(2,1)} %w_ref.1) | copy-start | bytes 1572868

commit v4 on v3

--- a/solution.py
+++ b/solution.py
@@ -14,6 +14,8 @@
 GROUP = QUERY_HEADS // KEY_VALUE_HEADS
 SCALE = 1.0 / math.sqrt(HEAD_SIZE)
 LOW = -(2.0**99)
+FAR = 18
+FAR_RANK = 4
 LIVE_BITS = 10
 
 VMEM = pl.BlockSpec(memory_space=pltpu.VMEM)
@@ -57,7 +59,7 @@
     out_ref[...] = jnp.broadcast_to(heads.astype(jnp.bfloat16)[None], out_ref.shape)
     score = SCALE * jnp.sum(heads * key[...].astype(jnp.float32), axis=-1, keepdims=True)
     device = lax.axis_index("attn")
-    own = lax.broadcasted_iota(jnp.int32, out_ref.shape, 0) == device
+    own = lax.broadcasted_iota(jnp.int32, out_ref.shape, 0) == device ^ FAR
     own_ref[0] = jnp.where(own, score[None], LOW)
     own_ref[1] = jnp.where(own, value[...].astype(jnp.float32)[None], 0.0)
 
@@ -68,7 +70,7 @@
     for r in range(lengths.shape[0]):
         length = jnp.where(row == r, lengths[r], length)
     start = lax.broadcasted_iota(jnp.int32, places.shape, 1) * BLOCK
-    code = (row << LIVE_BITS) + jnp.clip(length - start, 0, BLOCK)
+    code = ((row ^ FAR) << LIVE_BITS) + jnp.clip(length - start, 0, BLOCK)
     for slot in range(slots):
         code_ref[slot] = jnp.sum(jnp.where(places == slot, code, 0))
 
@@ -155,17 +157,29 @@
     width = total.shape[1] // ranks
     for rank in range(ranks):
         block = total[:, rank * width : (rank + 1) * width]
-        out_ref[rank] = jnp.concatenate(
+        out_ref[rank ^ FAR_RANK] = jnp.concatenate(
             [block[i * packed : (i + 1) * packed] for i in range(full // width)], axis=1
         )
 
 
 def sum_kernel(terms_ref, out_ref):
     total = jnp.sum(terms_ref[...], axis=0)
-    width = out_ref.shape[1]
-    out_ref[...] = jnp.concatenate(
-        [total[:, i * width : (i + 1) * width] for i in range(total.shape[1] // width)], axis=0
-    ).astype(jnp.bfloat16)
+    rows, width = out_ref.shape
+    packed = total.shape[0]
+    low = FAR % packed
+    step = low & -low
+    total = jnp.concatenate(
+        [total[i ^ low : (i ^ low) + step] for i in range(0, packed, step)], axis=0
+    )
+    blocks = [(i ^ FAR // packed) * width for i in range(rows // packed)]
+    out_ref[...] = jnp.concatenate([total[:, at : at + width] for at in blocks], axis=0).astype(
+        jnp.bfloat16
+    )
+
+
+def exchange(x, axis, far):
+    order = [i ^ far for i in range(lax.axis_size(axis))]
+    return lax.all_to_all(x, axis, 0, 0, tiled=True, axis_index_groups=[order])
 
 
 def in_hbm(x):
@@ -218,7 +232,7 @@
         ),
         name="spread",
     )(*map(in_hbm, (*small, key_cache_blocks, value_cache_blocks)))
-    every_query = lax.all_to_all(spread, "attn", 0, 0, tiled=True)
+    every_query = exchange(spread, "attn", FAR)
     state = pltpu.VMEM((rows, GROUP, 128), jnp.float32)
     partials = call(
         attention_kernel,
@@ -228,9 +242,9 @@
         [pltpu.VMEM((slots, GROUP, block), jnp.float32), state, state, state],
         4,
     )(codes, every_query, own, key_cache_blocks, value_cache_blocks)
-    partials = lax.all_to_all(partials, "attn", 0, 0, tiled=True)
+    partials = exchange(partials, "attn", FAR)
     attended = call(finish_kernel, "finish", per_row, [VMEM])(partials)
-    attended = lax.all_to_all(attended, "attn", 0, 0, tiled=True)
+    attended = exchange(attended, "attn", FAR)
 
     width = w_out.shape[1] // ranks
     terms = call(
@@ -241,7 +255,7 @@
         (),
         4,
     )(attended, w_out)
-    terms = lax.all_to_all(terms, "tensor", 0, 0, tiled=True)
+    terms = exchange(terms, "tensor", FAR_RANK)
     return call(sum_kernel, "sum", jax.ShapeDtypeStruct((rows, width), jnp.bfloat16), [VMEM])(terms)
 
 

time: 63.5 us -> 57 us (0.90)
  blocking collectives: 58.7 us -> 52.1 us
    all_to_all x4, blocking collectives: 58.7 us -> 52.1 us  [exchange(): return lax.all_to_all(x, axis, 0, 0, tiled=True, axis_index_groups=[order])]
where the time goes in v4:
time: 57 us; the launch traced here: 56.8 us
  blocking collectives  52.1 us (91%)
  Pallas kernels  4.61 us (8%)
    all_to_all x4, blocking collectives, exchange(): return lax.all_to_all(x, axis, 0, 0, tiled=True, axis_index_groups=[order])  52.1 us
    pallas_call x1, Pallas kernels, shards(): call(attention_kernel, 'attention', jax.ShapeDtypeStruct((rows, 2 * GROUP...  2.07 us
    pallas_call x1, Pallas kernels, shards(): pl.pallas_call(spread_kernel, out_shape=(per_row, jax.ShapeDtypeStruct((2...  1.31 us

profile of v4, /device:TPU:1, one launch (start us, length us, event | category | flops | bytes accessed | tf_op | source)
XLA Modules:
  0.0 56.8 jit_solution(255861412488013188)
XLA Ops:
  0.0 0.0 copy-start.1
  0.0 0.0 copy-start
  0.0 1.3 %spread.1 = (bf16[32,8,128]{2,1,0:T(8,128)(2,1)S(1)}, f32[2,32,8,128]{3,2,1,0:T(8,128)S(1)}, s32[32]{0:T(128)S(4)}) custom-call(bf16[1,1024]{1,0:T(2,128)(2,1)} %query_hbm.1, bf16[1,128]{1,0:T(2,128)(2,1)} %key_hbm.1, bf16[1,128]{1,0:T(2,128)(2,1)} %value_hbm.1, s32[32]{0:T(128)} %lengths_hbm.1, s32[32,249]{1,0:T(8,128)} %placement_hbm.1, ...), custom_call_target="tpu_custom_call" | custom-call | flops 1073741824 | bytes 67108864 | tf_op jit(solution)/shard_map/spread/pallas_call | solution.py:219
  1.3 16.3 %all_to_all.20.query_ref = bf16[32,8,128]{2,1,0:T(8,128)(2,1)S(1)} all-to-all(bf16[32,8,128]{2,1,0:T(8,128)(2,1)S(1)} %get-tuple-element.9), channel_id=1, replica_groups={{144,152,128,136,176,184,160,168,208,216,192,200,240,248,224,232,16,24,..., dimensions={0} | all-to-all | bytes 131072 | tf_op jit(solution)/shard_map/all_to_all | solution.py:182
  17.6 0.0 copy-done.1
  17.6 0.0 copy-done
  17.6 0.0 copy-start.2
  17.6 2.1 %attention.1 = bf16[32,16,128]{2,1,0:T(8,128)(2,1)S(1)} custom-call(s32[32]{0:T(128)S(4)} %get-tuple-element.8.code_ref, bf16[32,8,128]{2,1,0:T(8,128)(2,1)S(1)} %all_to_all.20.query_ref, f32[2,32,8,128]{3,2,1,0:T(8,128)S(1)} %get-tuple-element.10.own_ref, bf16[32,512,128]{2,1,0:T(8,128)(2,1)S(1)} %copy-done, bf16[32,512,128]{2,1,0:T(8,128)(2,1)S(1)} %copy-done.1), custom_call_target="tpu_custom_call" | custom-call | tf_op jit(solution)/shard_map/attention/pallas_call | solution.py:237
  19.7 12.6 %all_to_all.21.parts_ref = bf16[32,16,128]{2,1,0:T(8,128)(2,1)S(1)} all-to-all(bf16[32,16,128]{2,1,0:T(8,128)(2,1)S(1)} %attention.1), channel_id=1, replica_groups={{144,152,128,136,176,184,160,168,208,216,192,200,240,248,224,232,16,24,..., dimensions={0} | all-to-all | bytes 262144 | tf_op jit(solution)/shard_map/all_to_all | solution.py:182
  32.3 0.2 finish.1
  32.5 11.8 %all_to_all.22.attended_ref = bf16[32,8,128]{2,1,0:T(8,128)(2,1)S(1)} all-to-all(bf16[32,8,128]{2,1,0:T(8,128)(2,1)S(1)} %finish.1), channel_id=1, replica_groups={{144,152,128,136,176,184,160,168,208,216,192,200,240,248,224,232,16,24,..., dimensions={0} | all-to-all | bytes 131072 | tf_op jit(solution)/shard_map/all_to_all | solution.py:182
  44.3 0.0 copy-done.2
  44.3 0.3 project.1
  44.6 11.5 %all_to_all.23.terms_ref = f32[8,8,128]{2,1,0:T(8,128)S(1)} all-to-all(f32[8,8,128]{2,1,0:T(8,128)S(1)} %project.1), channel_id=1, replica_groups={{4,5,6,7,0,1,2,3},{12,13,14,15,8,9,10,11},{20,21,22,23,16,17,18,19},{28..., dimensions={0} | all-to-all | bytes 65536 | tf_op jit(solution)/shard_map/all_to_all | solution.py:182
  56.1 0.7 %sum.1 = bf16[32,32]{1,0:T(8,128)(2,1)} custom-call(f32[8,8,128]{2,1,0:T(8,128)S(1)} %all_to_all.23.terms_ref), custom_call_target="tpu_custom_call" | custom-call | tf_op jit(solution)/shard_map/sum/pallas_call | solution.py:259
Async XLA Ops:
  0.0 17.6 %copy-start.1 = (bf16[32,512,128]{2,1,0:T(8,128)(2,1)S(1)}, bf16[32,512,128]{2,1,0:T(8,128)(2,1)}, u32[]{:S(2)}) copy-start(bf16[32,512,128]{2,1,0:T(8,128)(2,1)} %value_ref.1) | copy-start | bytes 12582916
  0.0 17.6 %copy-start = (bf16[32,512,128]{2,1,0:T(8,128)(2,1)S(1)}, bf16[32,512,128]{2,1,0:T(8,128)(2,1)}, u32[]{:S(2)}) copy-start(bf16[32,512,128]{2,1,0:T(8,128)(2,1)} %key_ref.1) | copy-start | bytes 12582916
  17.6 26.7 %copy-start.2 = (bf16[1024,256]{1,0:T(8,128)(2,1)S(1)}, bf16[1024,256]{1,0:T(8,128)(2,1)}, u32[]{:S(2)}) copy-start(bf16[1024,256]{1,0:T(8,128)(2,1)} %w_ref.1) | copy-start | bytes 1572868

commit v5 on v4

--- a/solution.py
+++ b/solution.py
@@ -17,6 +17,7 @@
 FAR = 18
 FAR_RANK = 4
 LIVE_BITS = 10
+CODE_BITS = LIVE_BITS + 5
 
 VMEM = pl.BlockSpec(memory_space=pltpu.VMEM)
 SMEM = pl.BlockSpec(memory_space=pltpu.SMEM)
@@ -29,8 +30,6 @@
     value_hbm,
     lengths_hbm,
     placement_hbm,
-    key_cache_hbm,
-    value_cache_hbm,
     out_ref,
     own_ref,
     code_ref,
@@ -71,8 +70,15 @@
         length = jnp.where(row == r, lengths[r], length)
     start = lax.broadcasted_iota(jnp.int32, places.shape, 1) * BLOCK
     code = ((row ^ FAR) << LIVE_BITS) + jnp.clip(length - start, 0, BLOCK)
-    for slot in range(slots):
-        code_ref[slot] = jnp.sum(jnp.where(places == slot, code, 0))
+    high = code << CODE_BITS
+    for slot in range(0, slots, 2):
+        both = jnp.sum(jnp.where(places == slot, code, jnp.where(places == slot + 1, high, 0)))
+        code_ref[slot] = both & ((1 << CODE_BITS) - 1)
+        code_ref[slot + 1] = both >> CODE_BITS
+
+
+def hold_kernel(spread_ref, key_cache_hbm, value_cache_hbm, out_ref):
+    pass
 
 
 def attention_kernel(
@@ -113,9 +119,8 @@
     own_weight = jnp.exp(own_ref[0] - peaks[...])
     masses[...] = jnp.where(lane == 0, own_weight, 0.0)
     sums[...] = own_weight.astype(jnp.bfloat16).astype(jnp.float32) * own_ref[1]
-    for slot, (row, live) in enumerate(held):
+    for slot, (row, _) in enumerate(held):
         w = jnp.exp(scores[slot] - jnp.tile(peaks[row], (1, block // 128)))
-        w = jnp.where(position < live, w, 0.0)
         mass = w[:, :128]
         for part in range(1, block // 128):
             mass = mass + w[:, part * 128 : (part + 1) * 128]
@@ -144,7 +149,8 @@
 
 
 def project_kernel(attended_ref, w_ref, out_ref):
-    heads = jnp.swapaxes(attended_ref[...].astype(jnp.float32), 0, 1).astype(jnp.bfloat16)
+    rows = [attended_ref[row ^ FAR].astype(jnp.float32) for row in range(attended_ref.shape[0])]
+    heads = jnp.swapaxes(jnp.stack(rows), 0, 1).astype(jnp.bfloat16)
     total = None
     for head in range(GROUP):
         term = jnp.dot(
@@ -164,17 +170,10 @@
 
 def sum_kernel(terms_ref, out_ref):
     total = jnp.sum(terms_ref[...], axis=0)
-    rows, width = out_ref.shape
-    packed = total.shape[0]
-    low = FAR % packed
-    step = low & -low
-    total = jnp.concatenate(
-        [total[i ^ low : (i ^ low) + step] for i in range(0, packed, step)], axis=0
-    )
-    blocks = [(i ^ FAR // packed) * width for i in range(rows // packed)]
-    out_ref[...] = jnp.concatenate([total[:, at : at + width] for at in blocks], axis=0).astype(
-        jnp.bfloat16
-    )
+    width = out_ref.shape[1]
+    out_ref[...] = jnp.concatenate(
+        [total[:, i * width : (i + 1) * width] for i in range(total.shape[1] // width)], axis=0
+    ).astype(jnp.bfloat16)
 
 
 def exchange(x, axis, far):
@@ -223,15 +222,21 @@
             jax.ShapeDtypeStruct((2, *per_row.shape), jnp.float32),
             pltpu.SMEM((slots,), jnp.int32),
         ),
-        in_specs=[ANY] * (len(small) + 2),
+        in_specs=[ANY] * len(small),
         out_specs=(VMEM, VMEM, SMEM),
         scratch_shapes=room + [pltpu.SemaphoreType.DMA((len(small),))],
         compiler_params=pltpu.CompilerParams(vmem_limit_bytes=2 << 20),
-        cost_estimate=pl.CostEstimate(
-            flops=1 << 30, bytes_accessed=64 << 20, transcendentals=0
-        ),
         name="spread",
-    )(*map(in_hbm, (*small, key_cache_blocks, value_cache_blocks)))
+    )(*map(in_hbm, small))
+    spread = pl.pallas_call(
+        hold_kernel,
+        out_shape=per_row,
+        in_specs=[VMEM, ANY, ANY],
+        out_specs=VMEM,
+        input_output_aliases={0: 0},
+        compiler_params=pltpu.CompilerParams(vmem_limit_bytes=2 << 20),
+        name="hold",
+    )(spread, in_hbm(key_cache_blocks), in_hbm(value_cache_blocks))
     every_query = exchange(spread, "attn", FAR)
     state = pltpu.VMEM((rows, GROUP, 128), jnp.float32)
     partials = call(

time: 57 us -> 56.8 us (level)
  no operation moved by 1% of the time
where the time goes in v5:
time: 56.8 us; the launch traced here: 56.6 us
  blocking collectives  52.1 us (92%)
  Pallas kernels  4.36 us (8%)
    all_to_all x4, blocking collectives, exchange(): return lax.all_to_all(x, axis, 0, 0, tiled=True, axis_index_groups=[order])  52.1 us
    pallas_call x1, Pallas kernels, shards(): call(attention_kernel, 'attention', jax.ShapeDtypeStruct((rows, 2 * GROUP...  2.07 us

profile of v5, /device:TPU:1, one launch (start us, length us, event | category | flops | bytes accessed | tf_op | source)
XLA Modules:
  0.0 56.6 jit_solution(7185647681840781652)
XLA Ops:
  0.0 1.1 %spread.1 = (bf16[32,8,128]{2,1,0:T(8,128)(2,1)S(1)}, f32[2,32,8,128]{3,2,1,0:T(8,128)S(1)}, s32[32]{0:T(128)S(4)}) custom-call(bf16[1,1024]{1,0:T(2,128)(2,1)} %query_hbm.1, bf16[1,128]{1,0:T(2,128)(2,1)} %key_hbm.1, bf16[1,128]{1,0:T(2,128)(2,1)} %value_hbm.1, s32[32]{0:T(128)} %lengths_hbm.1, s32[32,249]{1,0:T(8,128)} %placement_hbm.1), custom_call_target="tpu_custom_call" | custom-call | tf_op jit(solution)/shard_map/spread/pallas_call | solution.py:218
  1.1 0.0 copy-start
  1.1 0.0 copy-start.1
  1.2 16.3 %all_to_all.20.query_ref = bf16[32,8,128]{2,1,0:T(8,128)(2,1)S(1)} all-to-all(bf16[32,8,128]{2,1,0:T(8,128)(2,1)S(1)} %hold.1), channel_id=1, replica_groups={{144,152,128,136,176,184,160,168,208,216,192,200,240,248,224,232,16,24,..., dimensions={0} | all-to-all | bytes 131072 | tf_op jit(solution)/shard_map/all_to_all | solution.py:181
  17.4 0.0 copy-done
  17.4 0.0 copy-done.1
  17.4 0.0 copy-start.2
  17.4 2.1 %attention.1 = bf16[32,16,128]{2,1,0:T(8,128)(2,1)S(1)} custom-call(s32[32]{0:T(128)S(4)} %get-tuple-element.8.code_ref, bf16[32,8,128]{2,1,0:T(8,128)(2,1)S(1)} %all_to_all.20.query_ref, f32[2,32,8,128]{3,2,1,0:T(8,128)S(1)} %get-tuple-element.10.own_ref, bf16[32,512,128]{2,1,0:T(8,128)(2,1)S(1)} %copy-done, bf16[32,512,128]{2,1,0:T(8,128)(2,1)S(1)} %copy-done.1), custom_call_target="tpu_custom_call" | custom-call | tf_op jit(solution)/shard_map/attention/pallas_call | solution.py:242
  19.5 12.6 %all_to_all.21.parts_ref = bf16[32,16,128]{2,1,0:T(8,128)(2,1)S(1)} all-to-all(bf16[32,16,128]{2,1,0:T(8,128)(2,1)S(1)} %attention.1), channel_id=1, replica_groups={{144,152,128,136,176,184,160,168,208,216,192,200,240,248,224,232,16,24,..., dimensions={0} | all-to-all | bytes 262144 | tf_op jit(solution)/shard_map/all_to_all | solution.py:181
  32.1 0.2 finish.1
  32.3 11.8 %all_to_all.22.attended_ref = bf16[32,8,128]{2,1,0:T(8,128)(2,1)S(1)} all-to-all(bf16[32,8,128]{2,1,0:T(8,128)(2,1)S(1)} %finish.1), channel_id=1, replica_groups={{144,152,128,136,176,184,160,168,208,216,192,200,240,248,224,232,16,24,..., dimensions={0} | all-to-all | bytes 131072 | tf_op jit(solution)/shard_map/all_to_all | solution.py:181
  44.1 0.0 copy-done.2
  44.2 0.3 project.1
  44.4 11.5 %all_to_all.23.terms_ref = f32[8,8,128]{2,1,0:T(8,128)S(1)} all-to-all(f32[8,8,128]{2,1,0:T(8,128)S(1)} %project.1), channel_id=1, replica_groups={{4,5,6,7,0,1,2,3},{12,13,14,15,8,9,10,11},{20,21,22,23,16,17,18,19},{28..., dimensions={0} | all-to-all | bytes 65536 | tf_op jit(solution)/shard_map/all_to_all | solution.py:181
  55.9 0.7 %sum.1 = bf16[32,32]{1,0:T(8,128)(2,1)} custom-call(f32[8,8,128]{2,1,0:T(8,128)S(1)} %all_to_all.23.terms_ref), custom_call_target="tpu_custom_call" | custom-call | tf_op jit(solution)/shard_map/sum/pallas_call | solution.py:264
  (1 shorter events, 0.0 us)
Async XLA Ops:
  1.1 16.3 %copy-start = (bf16[32,512,128]{2,1,0:T(8,128)(2,1)S(1)}, bf16[32,512,128]{2,1,0:T(8,128)(2,1)}, u32[]{:S(2)}) copy-start(bf16[32,512,128]{2,1,0:T(8,128)(2,1)} %key_ref.1) | copy-start | bytes 12582916
  1.1 16.3 %copy-start.1 = (bf16[32,512,128]{2,1,0:T(8,128)(2,1)S(1)}, bf16[32,512,128]{2,1,0:T(8,128)(2,1)}, u32[]{:S(2)}) copy-start(bf16[32,512,128]{2,1,0:T(8,128)(2,1)} %value_ref.1) | copy-start | bytes 12582916
  17.4 26.7 %copy-start.2 = (bf16[1024,256]{1,0:T(8,128)(2,1)S(1)}, bf16[1024,256]{1,0:T(8,128)(2,1)}, u32[]{:S(2)}) copy-start(bf16[1024,256]{1,0:T(8,128)(2,1)} %w_ref.1) | copy-start | bytes 1572868

commit v6 on v5

--- a/solution.py
+++ b/solution.py
@@ -16,6 +16,9 @@
 LOW = -(2.0**99)
 FAR = 18
 FAR_RANK = 4
+X = 4
+SETS = 2 * X
+FAR_SET = 6
 LIVE_BITS = 10
 CODE_BITS = LIVE_BITS + 5
 
@@ -130,26 +133,52 @@
         )
     mass = jnp.sum(masses[...], axis=-1, keepdims=True)
     high = mass.astype(jnp.bfloat16).astype(jnp.float32)
-    extra = jnp.where(lane == 0, peaks[...], jnp.where(lane == 1, high, mass - high))
-    out_ref[...] = jnp.concatenate([sums[...], extra], axis=1).astype(jnp.bfloat16)
+    low = mass - high
+    lane = lane[0]
+    share = rows // SETS
+    for which in range(SETS):
+        extra = jnp.zeros((GROUP, 128), jnp.float32)
+        for i in range(share):
+            place, at = which * share + i, i * (128 // share)
+            extra = jnp.where(lane == at, peaks[place], extra)
+            extra = jnp.where(lane == at + 1, high[place], extra)
+            extra = jnp.where(lane == at + 2, low[place], extra)
+        block = sums[which * share : (which + 1) * share].reshape(share * GROUP, 128)
+        block = jnp.concatenate([block, extra], axis=0).astype(jnp.bfloat16)
+        for place in range(out_ref.shape[0]):
+            if set_of(place ^ FAR) == which:
+                out_ref[place] = block
+
+
+def set_of(device):
+    return device // X % 2 * X + device % X
 
 
 def finish_kernel(parts_ref, out_ref):
     parts = parts_ref[...].astype(jnp.float32)
-    partial = parts[:, :GROUP]
-    extra = parts[:, GROUP:]
-    peaks = extra[:, :, 0:1]
-    highest = jnp.max(peaks, axis=0, keepdims=True)
-    factor = jnp.exp(peaks - highest)
-    masses = extra[:, :, 1:2] + extra[:, :, 2:3]
-    denominator = jnp.sum(masses * factor, axis=0)
-    total = jnp.sum(partial * factor, axis=0)
-    attended = (total / denominator).astype(jnp.bfloat16)
+    share = parts.shape[1] // GROUP - 1
+    extra = parts[:, share * GROUP :]
+    attended = []
+    for i in range(share):
+        partial = parts[:, i * GROUP : (i + 1) * GROUP]
+        at = i * (128 // share)
+        peaks = extra[:, :, at : at + 1]
+        highest = jnp.max(peaks, axis=0, keepdims=True)
+        factor = jnp.exp(peaks - highest)
+        masses = extra[:, :, at + 1 : at + 2] + extra[:, :, at + 2 : at + 3]
+        denominator = jnp.sum(masses * factor, axis=0)
+        attended.append(jnp.sum(partial * factor, axis=0) / denominator)
+    attended = jnp.concatenate(attended, axis=0).astype(jnp.bfloat16)
     out_ref[...] = jnp.broadcast_to(attended[None], out_ref.shape)
 
 
 def project_kernel(attended_ref, w_ref, out_ref):
-    rows = [attended_ref[row ^ FAR].astype(jnp.float32) for row in range(attended_ref.shape[0])]
+    sets = attended_ref[...].astype(jnp.float32)
+    share = sets.shape[1] // GROUP
+    rows = []
+    for place in (row ^ FAR for row in range(SETS * share)):
+        at = place % share * GROUP
+        rows.append(sets[place // share ^ FAR_SET, at : at + GROUP])
     heads = jnp.swapaxes(jnp.stack(rows), 0, 1).astype(jnp.bfloat16)
     total = None
     for head in range(GROUP):
@@ -176,9 +205,8 @@
     ).astype(jnp.bfloat16)
 
 
-def exchange(x, axis, far):
-    order = [i ^ far for i in range(lax.axis_size(axis))]
-    return lax.all_to_all(x, axis, 0, 0, tiled=True, axis_index_groups=[order])
+def exchange(x, axis, groups):
+    return lax.all_to_all(x, axis, 0, 0, tiled=True, axis_index_groups=groups)
 
 
 def in_hbm(x):
@@ -210,6 +238,9 @@
     rows = lengths.shape[0]
     slots, block, _ = key_cache_blocks.shape
     ranks = lax.axis_size("tensor")
+    everyone = [[i ^ FAR for i in range(rows)]]
+    blocks = [[at + (i ^ FAR_SET) for i in range(SETS)] for at in range(0, rows, SETS)]
+    share = rows // SETS * GROUP
     per_row = jax.ShapeDtypeStruct((rows, GROUP, HEAD_SIZE), jnp.bfloat16)
 
     small = (queries, fresh_keys, fresh_values, lengths, placement)
@@ -237,19 +268,24 @@
         compiler_params=pltpu.CompilerParams(vmem_limit_bytes=2 << 20),
         name="hold",
     )(spread, in_hbm(key_cache_blocks), in_hbm(value_cache_blocks))
-    every_query = exchange(spread, "attn", FAR)
+    every_query = exchange(spread, "attn", everyone)
     state = pltpu.VMEM((rows, GROUP, 128), jnp.float32)
     partials = call(
         attention_kernel,
         "attention",
-        jax.ShapeDtypeStruct((rows, 2 * GROUP, HEAD_SIZE), jnp.bfloat16),
+        jax.ShapeDtypeStruct((rows, share + GROUP, HEAD_SIZE), jnp.bfloat16),
         [SMEM, VMEM, VMEM, VMEM, VMEM],
         [pltpu.VMEM((slots, GROUP, block), jnp.float32), state, state, state],
         4,
     )(codes, every_query, own, key_cache_blocks, value_cache_blocks)
-    partials = exchange(partials, "attn", FAR)
-    attended = call(finish_kernel, "finish", per_row, [VMEM])(partials)
-    attended = exchange(attended, "attn", FAR)
+    partials = exchange(partials, "attn", everyone)
+    attended = call(
+        finish_kernel,
+        "finish",
+        jax.ShapeDtypeStruct((SETS, share, HEAD_SIZE), jnp.bfloat16),
+        [VMEM],
+    )(partials)
+    attended = exchange(attended, "attn", blocks)
 
     width = w_out.shape[1] // ranks
     terms = call(
@@ -260,7 +296,7 @@
         (),
         4,
     )(attended, w_out)
-    terms = exchange(terms, "tensor", FAR_RANK)
+    terms = exchange(terms, "tensor", [[i ^ FAR_RANK for i in range(ranks)]])
     return call(sum_kernel, "sum", jax.ShapeDtypeStruct((rows, width), jnp.bfloat16), [VMEM])(terms)
 
 

time: 56.8 us -> 55.9 us (0.984)
  blocking collectives: 52.1 us -> 50.9 us
    all_to_all x4, blocking collectives: 52.1 us -> 50.9 us  [exchange(): return lax.all_to_all(x, axis, 0, 0, tiled=True, axis_index_groups=groups)]
where the time goes in v6:
time: 55.9 us; the launch traced here: 55.6 us
  blocking collectives  50.9 us (91%)
  Pallas kernels  4.62 us (8%)
    all_to_all x4, blocking collectives, exchange(): return lax.all_to_all(x, axis, 0, 0, tiled=True, axis_index_groups=groups)  50.9 us
    pallas_call x1, Pallas kernels, shards(): call(attention_kernel, 'attention', jax.ShapeDtypeStruct((rows, share + G...  2.09 us
    pallas_call x1, Pallas kernels, shards(): pl.pallas_call(spread_kernel, out_shape=(per_row, jax.ShapeDtypeStruct((2...  1.12 us

profile of v6, /device:TPU:1, one launch (start us, length us, event | category | flops | bytes accessed | tf_op | source)
XLA Modules:
  0.0 55.6 jit_solution(16784587181492453493)
XLA Ops:
  0.0 1.1 %spread.1 = (bf16[32,8,128]{2,1,0:T(8,128)(2,1)S(1)}, f32[2,32,8,128]{3,2,1,0:T(8,128)S(1)}, s32[32]{0:T(128)S(4)}) custom-call(bf16[1,1024]{1,0:T(2,128)(2,1)} %query_hbm.1, bf16[1,128]{1,0:T(2,128)(2,1)} %key_hbm.1, bf16[1,128]{1,0:T(2,128)(2,1)} %value_hbm.1, s32[32]{0:T(128)} %lengths_hbm.1, s32[32,249]{1,0:T(8,128)} %placement_hbm.1), custom_call_target="tpu_custom_call" | custom-call | tf_op jit(solution)/shard_map/spread/pallas_call | solution.py:249
  1.1 0.0 copy-start
  1.1 0.0 copy-start.1
  1.2 16.3 %all_to_all.20.query_ref = bf16[32,8,128]{2,1,0:T(8,128)(2,1)S(1)} all-to-all(bf16[32,8,128]{2,1,0:T(8,128)(2,1)S(1)} %hold.1), channel_id=1, replica_groups={{144,152,128,136,176,184,160,168,208,216,192,200,240,248,224,232,16,24,..., dimensions={0} | all-to-all | bytes 131072 | tf_op jit(solution)/shard_map/all_to_all | solution.py:209
  17.4 0.0 copy-done
  17.4 0.0 copy-done.1
  17.4 0.0 copy-start.2
  17.4 2.1 %attention.1 = bf16[32,40,128]{2,1,0:T(8,128)(2,1)S(1)} custom-call(s32[32]{0:T(128)S(4)} %get-tuple-element.8.code_ref, bf16[32,8,128]{2,1,0:T(8,128)(2,1)S(1)} %all_to_all.20.query_ref, f32[2,32,8,128]{3,2,1,0:T(8,128)S(1)} %get-tuple-element.10.own_ref, bf16[32,512,128]{2,1,0:T(8,128)(2,1)S(1)} %copy-done, bf16[32,512,128]{2,1,0:T(8,128)(2,1)S(1)} %copy-done.1), custom_call_target="tpu_custom_call" | custom-call | tf_op jit(solution)/shard_map/attention/pallas_call | solution.py:273
  19.5 16.2 %all_to_all.21.parts_ref = bf16[32,40,128]{2,1,0:T(8,128)(2,1)S(1)} all-to-all(bf16[32,40,128]{2,1,0:T(8,128)(2,1)S(1)} %attention.1), channel_id=1, replica_groups={{144,152,128,136,176,184,160,168,208,216,192,200,240,248,224,232,16,24,..., dimensions={0} | all-to-all | bytes 655360 | tf_op jit(solution)/shard_map/all_to_all | solution.py:209
  35.8 0.5 finish.1
  36.2 6.7 %all_to_all.22.attended_ref = bf16[8,32,128]{2,1,0:T(8,128)(2,1)S(1)} all-to-all(bf16[8,32,128]{2,1,0:T(8,128)(2,1)S(1)} %finish.1), channel_id=1, replica_groups={{48,56,32,40,16,24,0,8},{112,120,96,104,80,88,64,72},{176,184,160,168,1..., dimensions={0} | all-to-all | bytes 131072 | tf_op jit(solution)/shard_map/all_to_all | solution.py:209
  43.0 0.0 copy-done.2
  43.0 0.3 project.1
  43.2 11.7 %all_to_all.23.terms_ref = f32[8,8,128]{2,1,0:T(8,128)S(1)} all-to-all(f32[8,8,128]{2,1,0:T(8,128)S(1)} %project.1), channel_id=1, replica_groups={{4,5,6,7,0,1,2,3},{12,13,14,15,8,9,10,11},{20,21,22,23,16,17,18,19},{28..., dimensions={0} | all-to-all | bytes 65536 | tf_op jit(solution)/shard_map/all_to_all | solution.py:209
  54.9 0.7 %sum.1 = bf16[32,32]{1,0:T(8,128)(2,1)} custom-call(f32[8,8,128]{2,1,0:T(8,128)S(1)} %all_to_all.23.terms_ref), custom_call_target="tpu_custom_call" | custom-call | tf_op jit(solution)/shard_map/sum/pallas_call | solution.py:300
  (1 shorter events, 0.0 us)
Async XLA Ops:
  1.1 16.3 %copy-start = (bf16[32,512,128]{2,1,0:T(8,128)(2,1)S(1)}, bf16[32,512,128]{2,1,0:T(8,128)(2,1)}, u32[]{:S(2)}) copy-start(bf16[32,512,128]{2,1,0:T(8,128)(2,1)} %key_ref.1) | copy-start | bytes 12582916
  1.1 16.3 %copy-start.1 = (bf16[32,512,128]{2,1,0:T(8,128)(2,1)S(1)}, bf16[32,512,128]{2,1,0:T(8,128)(2,1)}, u32[]{:S(2)}) copy-start(bf16[32,512,128]{2,1,0:T(8,128)(2,1)} %value_ref.1) | copy-start | bytes 12582916
  17.4 25.5 %copy-start.2 = (bf16[1024,256]{1,0:T(8,128)(2,1)S(1)}, bf16[1024,256]{1,0:T(8,128)(2,1)}, u32[]{:S(2)}) copy-start(bf16[1024,256]{1,0:T(8,128)(2,1)} %w_ref.1) | copy-start | bytes 1572868

commit v7 on v6

--- a/solution.py
+++ b/solution.py
@@ -14,9 +14,18 @@
 GROUP = QUERY_HEADS // KEY_VALUE_HEADS
 SCALE = 1.0 / math.sqrt(HEAD_SIZE)
 LOW = -(2.0**99)
-FAR = 18
 FAR_RANK = 4
+Z = 8
 X = 4
+
+
+def hops(device):
+    return abs(device // X - Z // 2) + abs(device % X - X // 2)
+
+
+ORDER = sorted(range(Z * X), key=lambda device: (hops(device), device))
+PLACE = [ORDER.index(device) for device in range(Z * X)]
+
 SETS = 2 * X
 FAR_SET = 6
 LIVE_BITS = 10
@@ -61,18 +70,22 @@
     out_ref[...] = jnp.broadcast_to(heads.astype(jnp.bfloat16)[None], out_ref.shape)
     score = SCALE * jnp.sum(heads * key[...].astype(jnp.float32), axis=-1, keepdims=True)
     device = lax.axis_index("attn")
-    own = lax.broadcasted_iota(jnp.int32, out_ref.shape, 0) == device ^ FAR
-    own_ref[0] = jnp.where(own, score[None], LOW)
-    own_ref[1] = jnp.where(own, value[...].astype(jnp.float32)[None], 0.0)
+    score = jnp.broadcast_to(score, (GROUP, HEAD_SIZE))
+    fresh = jnp.broadcast_to(value[...].astype(jnp.float32), (GROUP, HEAD_SIZE))
+    for place, owner in enumerate(ORDER):
+        own_ref[0, place] = jnp.where(device == owner, score, LOW)
+        own_ref[1, place] = jnp.where(device == owner, fresh, 0.0)
 
     slots = code_ref.shape[0]
     places = placement[...] - device * slots
     row = lax.broadcasted_iota(jnp.int32, places.shape, 0)
     length = jnp.zeros_like(places)
+    place = jnp.zeros_like(places)
     for r in range(lengths.shape[0]):
         length = jnp.where(row == r, lengths[r], length)
+        place = jnp.where(row == r, PLACE[r], place)
     start = lax.broadcasted_iota(jnp.int32, places.shape, 1) * BLOCK
-    code = ((row ^ FAR) << LIVE_BITS) + jnp.clip(length - start, 0, BLOCK)
+    code = (place << LIVE_BITS) + jnp.clip(length - start, 0, BLOCK)
     high = code << CODE_BITS
     for slot in range(0, slots, 2):
         both = jnp.sum(jnp.where(places == slot, code, jnp.where(places == slot + 1, high, 0)))
@@ -146,7 +159,7 @@
         block = sums[which * share : (which + 1) * share].reshape(share * GROUP, 128)
         block = jnp.concatenate([block, extra], axis=0).astype(jnp.bfloat16)
         for place in range(out_ref.shape[0]):
-            if set_of(place ^ FAR) == which:
+            if set_of(ORDER[place]) == which:
                 out_ref[place] = block
 
 
@@ -158,16 +171,14 @@
     parts = parts_ref[...].astype(jnp.float32)
     share = parts.shape[1] // GROUP - 1
     extra = parts[:, share * GROUP :]
+    factor = jnp.exp(extra - jnp.max(extra, axis=0, keepdims=True))
+    masses = pltpu.roll(extra, 127, 2) + pltpu.roll(extra, 126, 2)
+    factor = factor / jnp.sum(masses * factor, axis=0, keepdims=True)
     attended = []
     for i in range(share):
+        at = i * (128 // share)
         partial = parts[:, i * GROUP : (i + 1) * GROUP]
-        at = i * (128 // share)
-        peaks = extra[:, :, at : at + 1]
-        highest = jnp.max(peaks, axis=0, keepdims=True)
-        factor = jnp.exp(peaks - highest)
-        masses = extra[:, :, at + 1 : at + 2] + extra[:, :, at + 2 : at + 3]
-        denominator = jnp.sum(masses * factor, axis=0)
-        attended.append(jnp.sum(partial * factor, axis=0) / denominator)
+        attended.append(jnp.sum(partial * factor[:, :, at : at + 1], axis=0))
     attended = jnp.concatenate(attended, axis=0).astype(jnp.bfloat16)
     out_ref[...] = jnp.broadcast_to(attended[None], out_ref.shape)
 
@@ -176,7 +187,7 @@
     sets = attended_ref[...].astype(jnp.float32)
     share = sets.shape[1] // GROUP
     rows = []
-    for place in (row ^ FAR for row in range(SETS * share)):
+    for place in PLACE:
         at = place % share * GROUP
         rows.append(sets[place // share ^ FAR_SET, at : at + GROUP])
     heads = jnp.swapaxes(jnp.stack(rows), 0, 1).astype(jnp.bfloat16)
@@ -238,7 +249,7 @@
     rows = lengths.shape[0]
     slots, block, _ = key_cache_blocks.shape
     ranks = lax.axis_size("tensor")
-    everyone = [[i ^ FAR for i in range(rows)]]
+    everyone = [ORDER]
     blocks = [[at + (i ^ FAR_SET) for i in range(SETS)] for at in range(0, rows, SETS)]
     share = rows // SETS * GROUP
     per_row = jax.ShapeDtypeStruct((rows, GROUP, HEAD_SIZE), jnp.bfloat16)

time: 55.9 us -> 55.4 us (level)
  no operation moved by 1% of the time
where the time goes in v7:
time: 55.4 us; the launch traced here: 55.2 us
  blocking collectives  50.6 us (91%)
  Pallas kernels  4.52 us (8%)
    all_to_all x4, blocking collectives, exchange(): return lax.all_to_all(x, axis, 0, 0, tiled=True, axis_index_groups=groups)  50.6 us
    pallas_call x1, Pallas kernels, shards(): call(attention_kernel, 'attention', jax.ShapeDtypeStruct((rows, share + G...  2.1 us
    pallas_call x1, Pallas kernels, shards(): pl.pallas_call(spread_kernel, out_shape=(per_row, jax.ShapeDtypeStruct((2...  1.12 us

profile of v7, /device:TPU:1, one launch (start us, length us, event | category | flops | bytes accessed | tf_op | source)
XLA Modules:
  0.0 55.2 jit_solution(3501745191643343959)
XLA Ops:
  0.0 1.1 %spread.1 = (bf16[32,8,128]{2,1,0:T(8,128)(2,1)S(1)}, f32[2,32,8,128]{3,2,1,0:T(8,128)S(1)}, s32[32]{0:T(128)S(4)}) custom-call(bf16[1,1024]{1,0:T(2,128)(2,1)} %query_hbm.1, bf16[1,128]{1,0:T(2,128)(2,1)} %key_hbm.1, bf16[1,128]{1,0:T(2,128)(2,1)} %value_hbm.1, s32[32]{0:T(128)} %lengths_hbm.1, s32[32,249]{1,0:T(8,128)} %placement_hbm.1), custom_call_target="tpu_custom_call" | custom-call | tf_op jit(solution)/shard_map/spread/pallas_call | solution.py:260
  1.1 0.0 copy-start
  1.1 0.0 copy-start.1
  1.2 16.2 %all_to_all.20.query_ref = bf16[32,8,128]{2,1,0:T(8,128)(2,1)S(1)} all-to-all(bf16[32,8,128]{2,1,0:T(8,128)(2,1)S(1)} %hold.1), channel_id=1, replica_groups={{144,112,136,152,176,80,104,120,128,168,184,208,48,72,88,96,160,200,216..., dimensions={0} | all-to-all | bytes 131072 | tf_op jit(solution)/shard_map/all_to_all | solution.py:220
  17.4 0.0 copy-done
  17.4 0.0 copy-done.1
  17.4 0.0 copy-start.2
  17.4 2.1 %attention.1 = bf16[32,40,128]{2,1,0:T(8,128)(2,1)S(1)} custom-call(s32[32]{0:T(128)S(4)} %get-tuple-element.8.code_ref, bf16[32,8,128]{2,1,0:T(8,128)(2,1)S(1)} %all_to_all.20.query_ref, f32[2,32,8,128]{3,2,1,0:T(8,128)S(1)} %get-tuple-element.10.own_ref, bf16[32,512,128]{2,1,0:T(8,128)(2,1)S(1)} %copy-done, bf16[32,512,128]{2,1,0:T(8,128)(2,1)S(1)} %copy-done.1), custom_call_target="tpu_custom_call" | custom-call | tf_op jit(solution)/shard_map/attention/pallas_call | solution.py:284
  19.5 16.4 %all_to_all.21.parts_ref = bf16[32,40,128]{2,1,0:T(8,128)(2,1)S(1)} all-to-all(bf16[32,40,128]{2,1,0:T(8,128)(2,1)S(1)} %attention.1), channel_id=1, replica_groups={{144,112,136,152,176,80,104,120,128,168,184,208,48,72,88,96,160,200,216..., dimensions={0} | all-to-all | bytes 655360 | tf_op jit(solution)/shard_map/all_to_all | solution.py:220
  35.9 0.3 finish.1
  36.3 7.3 %all_to_all.22.attended_ref = bf16[8,32,128]{2,1,0:T(8,128)(2,1)S(1)} all-to-all(bf16[8,32,128]{2,1,0:T(8,128)(2,1)S(1)} %finish.1), channel_id=1, replica_groups={{48,56,32,40,16,24,0,8},{112,120,96,104,80,88,64,72},{176,184,160,168,1..., dimensions={0} | all-to-all | bytes 131072 | tf_op jit(solution)/shard_map/all_to_all | solution.py:220
  43.6 0.0 copy-done.2
  43.6 0.3 project.1
  43.8 10.6 %all_to_all.23.terms_ref = f32[8,8,128]{2,1,0:T(8,128)S(1)} all-to-all(f32[8,8,128]{2,1,0:T(8,128)S(1)} %project.1), channel_id=1, replica_groups={{4,5,6,7,0,1,2,3},{12,13,14,15,8,9,10,11},{20,21,22,23,16,17,18,19},{28..., dimensions={0} | all-to-all | bytes 65536 | tf_op jit(solution)/shard_map/all_to_all | solution.py:220
  54.5 0.7 %sum.1 = bf16[32,32]{1,0:T(8,128)(2,1)} custom-call(f32[8,8,128]{2,1,0:T(8,128)S(1)} %all_to_all.23.terms_ref), custom_call_target="tpu_custom_call" | custom-call | tf_op jit(solution)/shard_map/sum/pallas_call | solution.py:311
  (1 shorter events, 0.0 us)
Async XLA Ops:
  1.1 16.3 %copy-start = (bf16[32,512,128]{2,1,0:T(8,128)(2,1)S(1)}, bf16[32,512,128]{2,1,0:T(8,128)(2,1)}, u32[]{:S(2)}) copy-start(bf16[32,512,128]{2,1,0:T(8,128)(2,1)} %key_ref.1) | copy-start | bytes 12582916
  1.1 16.3 %copy-start.1 = (bf16[32,512,128]{2,1,0:T(8,128)(2,1)S(1)}, bf16[32,512,128]{2,1,0:T(8,128)(2,1)}, u32[]{:S(2)}) copy-start(bf16[32,512,128]{2,1,0:T(8,128)(2,1)} %value_ref.1) | copy-start | bytes 12582916
  17.4 26.2 %copy-start.2 = (bf16[1024,256]{1,0:T(8,128)(2,1)S(1)}, bf16[1024,256]{1,0:T(8,128)(2,1)}, u32[]{:S(2)}) copy-start(bf16[1024,256]{1,0:T(8,128)(2,1)} %w_ref.1) | copy-start | bytes 1572868

commit v8 on v7

--- a/solution.py
+++ b/solution.py
@@ -62,7 +62,7 @@
     copies = [pltpu.make_async_copy(*pair, sems.at[i]) for i, pair in enumerate(pairs)]
     for copy in copies:
         copy.start()
-    for copy in copies:
+    for copy in copies[:3]:
         copy.wait()
     wide = query[...].astype(jnp.float32)
     heads = [wide[:, head * HEAD_SIZE : (head + 1) * HEAD_SIZE] for head in range(GROUP)]
@@ -76,6 +76,8 @@
         own_ref[0, place] = jnp.where(device == owner, score, LOW)
         own_ref[1, place] = jnp.where(device == owner, fresh, 0.0)
 
+    for copy in copies[3:]:
+        copy.wait()
     slots = code_ref.shape[0]
     places = placement[...] - device * slots
     row = lax.broadcasted_iota(jnp.int32, places.shape, 0)
@@ -205,11 +207,11 @@
         block = total[:, rank * width : (rank + 1) * width]
         out_ref[rank ^ FAR_RANK] = jnp.concatenate(
             [block[i * packed : (i + 1) * packed] for i in range(full // width)], axis=1
-        )
+        ).astype(out_ref.dtype)
 
 
 def sum_kernel(terms_ref, out_ref):
-    total = jnp.sum(terms_ref[...], axis=0)
+    total = jnp.sum(terms_ref[...].astype(jnp.float32), axis=0)
     width = out_ref.shape[1]
     out_ref[...] = jnp.concatenate(
         [total[:, i * width : (i + 1) * width] for i in range(total.shape[1] // width)], axis=0
@@ -302,7 +304,7 @@
     terms = call(
         project_kernel,
         "project",
-        jax.ShapeDtypeStruct((ranks, rows * width // 128, 128), jnp.float32),
+        jax.ShapeDtypeStruct((ranks, rows * width // 128, 128), jnp.bfloat16),
         [VMEM, VMEM],
         (),
         4,

time: 55.4 us -> 55.4 us (level)
  no operation moved by 1% of the time
where the time goes in v8:
time: 55.4 us; the launch traced here: 55.1 us
  blocking collectives  50.6 us (91%)
  Pallas kernels  4.5 us (8%)
    all_to_all x4, blocking collectives, exchange(): return lax.all_to_all(x, axis, 0, 0, tiled=True, axis_index_groups=groups)  50.6 us
    pallas_call x1, Pallas kernels, shards(): call(attention_kernel, 'attention', jax.ShapeDtypeStruct((rows, share + G...  2.09 us
    pallas_call x1, Pallas kernels, shards(): pl.pallas_call(spread_kernel, out_shape=(per_row, jax.ShapeDtypeStruct((2...  1.12 us

profile of v8, /device:TPU:1, one launch (start us, length us, event | category | flops | bytes accessed | tf_op | source)
XLA Modules:
  0.0 55.1 jit_solution(12049981683840500398)
XLA Ops:
  0.0 1.1 %spread.1 = (bf16[32,8,128]{2,1,0:T(8,128)(2,1)S(1)}, f32[2,32,8,128]{3,2,1,0:T(8,128)S(1)}, s32[32]{0:T(128)S(4)}) custom-call(bf16[1,1024]{1,0:T(2,128)(2,1)} %query_hbm.1, bf16[1,128]{1,0:T(2,128)(2,1)} %key_hbm.1, bf16[1,128]{1,0:T(2,128)(2,1)} %value_hbm.1, s32[32]{0:T(128)} %lengths_hbm.1, s32[32,249]{1,0:T(8,128)} %placement_hbm.1), custom_call_target="tpu_custom_call" | custom-call | tf_op jit(solution)/shard_map/spread/pallas_call | solution.py:262
  1.1 0.0 copy-start
  1.1 0.0 copy-start.1
  1.2 16.2 %all_to_all.20.query_ref = bf16[32,8,128]{2,1,0:T(8,128)(2,1)S(1)} all-to-all(bf16[32,8,128]{2,1,0:T(8,128)(2,1)S(1)} %hold.1), channel_id=1, replica_groups={{144,112,136,152,176,80,104,120,128,168,184,208,48,72,88,96,160,200,216..., dimensions={0} | all-to-all | bytes 131072 | tf_op jit(solution)/shard_map/all_to_all | solution.py:222
  17.4 0.0 copy-done
  17.4 0.0 copy-done.1
  17.4 0.0 copy-start.2
  17.4 2.1 %attention.1 = bf16[32,40,128]{2,1,0:T(8,128)(2,1)S(1)} custom-call(s32[32]{0:T(128)S(4)} %get-tuple-element.8.code_ref, bf16[32,8,128]{2,1,0:T(8,128)(2,1)S(1)} %all_to_all.20.query_ref, f32[2,32,8,128]{3,2,1,0:T(8,128)S(1)} %get-tuple-element.10.own_ref, bf16[32,512,128]{2,1,0:T(8,128)(2,1)S(1)} %copy-done, bf16[32,512,128]{2,1,0:T(8,128)(2,1)S(1)} %copy-done.1), custom_call_target="tpu_custom_call" | custom-call | tf_op jit(solution)/shard_map/attention/pallas_call | solution.py:286
  19.5 16.4 %all_to_all.21.parts_ref = bf16[32,40,128]{2,1,0:T(8,128)(2,1)S(1)} all-to-all(bf16[32,40,128]{2,1,0:T(8,128)(2,1)S(1)} %attention.1), channel_id=1, replica_groups={{144,112,136,152,176,80,104,120,128,168,184,208,48,72,88,96,160,200,216..., dimensions={0} | all-to-all | bytes 655360 | tf_op jit(solution)/shard_map/all_to_all | solution.py:222
  35.9 0.3 finish.1
  36.3 7.3 %all_to_all.22.attended_ref = bf16[8,32,128]{2,1,0:T(8,128)(2,1)S(1)} all-to-all(bf16[8,32,128]{2,1,0:T(8,128)(2,1)S(1)} %finish.1), channel_id=1, replica_groups={{48,56,32,40,16,24,0,8},{112,120,96,104,80,88,64,72},{176,184,160,168,1..., dimensions={0} | all-to-all | bytes 131072 | tf_op jit(solution)/shard_map/all_to_all | solution.py:222
  43.5 0.0 copy-done.2
  43.5 0.3 project.1
  43.8 10.6 %all_to_all.23.terms_ref = bf16[8,8,128]{2,1,0:T(8,128)(2,1)S(1)} all-to-all(bf16[8,8,128]{2,1,0:T(8,128)(2,1)S(1)} %project.1), channel_id=1, replica_groups={{4,5,6,7,0,1,2,3},{12,13,14,15,8,9,10,11},{20,21,22,23,16,17,18,19},{28..., dimensions={0} | all-to-all | bytes 32768 | tf_op jit(solution)/shard_map/all_to_all | solution.py:222
  54.4 0.7 %sum.1 = bf16[32,32]{1,0:T(8,128)(2,1)} custom-call(bf16[8,8,128]{2,1,0:T(8,128)(2,1)S(1)} %all_to_all.23.terms_ref), custom_call_target="tpu_custom_call" | custom-call | tf_op jit(solution)/shard_map/sum/pallas_call | solution.py:313
  (1 shorter events, 0.0 us)
Async XLA Ops:
  1.1 16.3 %copy-start = (bf16[32,512,128]{2,1,0:T(8,128)(2,1)S(1)}, bf16[32,512,128]{2,1,0:T(8,128)(2,1)}, u32[]{:S(2)}) copy-start(bf16[32,512,128]{2,1,0:T(8,128)(2,1)} %key_ref.1) | copy-start | bytes 12582916
  1.1 16.3 %copy-start.1 = (bf16[32,512,128]{2,1,0:T(8,128)(2,1)S(1)}, bf16[32,512,128]{2,1,0:T(8,128)(2,1)}, u32[]{:S(2)}) copy-start(bf16[32,512,128]{2,1,0:T(8,128)(2,1)} %value_ref.1) | copy-start | bytes 12582916
  17.4 26.1 %copy-start.2 = (bf16[1024,256]{1,0:T(8,128)(2,1)S(1)}, bf16[1024,256]{1,0:T(8,128)(2,1)}, u32[]{:S(2)}) copy-start(bf16[1024,256]{1,0:T(8,128)(2,1)} %w_ref.1) | copy-start | bytes 1572868

commit v9 on v7

--- a/solution.py
+++ b/solution.py
@@ -16,11 +16,13 @@
 LOW = -(2.0**99)
 FAR_RANK = 4
 Z = 8
+FAR_Z = 5
 X = 4
 
 
 def hops(device):
-    return abs(device // X - Z // 2) + abs(device % X - X // 2)
+    along_z = (device // X - FAR_Z) % Z
+    return min(along_z, Z - along_z) + abs(device % X - X // 2)
 
 
 ORDER = sorted(range(Z * X), key=lambda device: (hops(device), device))

time: 55.4 us -> 55.2 us (level)
  no operation moved by 1% of the time
where the time goes in v9:
time: 55.2 us; the launch traced here: 55 us
  blocking collectives  50.4 us (91%)
  Pallas kernels  4.5 us (8%)
    all_to_all x4, blocking collectives, exchange(): return lax.all_to_all(x, axis, 0, 0, tiled=True, axis_index_groups=groups)  50.4 us
    pallas_call x1, Pallas kernels, shards(): call(attention_kernel, 'attention', jax.ShapeDtypeStruct((rows, share + G...  2.08 us
    pallas_call x1, Pallas kernels, shards(): pl.pallas_call(spread_kernel, out_shape=(per_row, jax.ShapeDtypeStruct((2...  1.12 us

profile of v9, /device:TPU:1, one launch (start us, length us, event | category | flops | bytes accessed | tf_op | source)
XLA Modules:
  0.0 55.0 jit_solution(2786217772526708038)
XLA Ops:
  0.0 1.1 %spread.1 = (bf16[32,8,128]{2,1,0:T(8,128)(2,1)S(1)}, f32[2,32,8,128]{3,2,1,0:T(8,128)S(1)}, s32[32]{0:T(128)S(4)}) custom-call(bf16[1,1024]{1,0:T(2,128)(2,1)} %query_hbm.1, bf16[1,128]{1,0:T(2,128)(2,1)} %key_hbm.1, bf16[1,128]{1,0:T(2,128)(2,1)} %value_hbm.1, s32[32]{0:T(128)} %lengths_hbm.1, s32[32,249]{1,0:T(8,128)} %placement_hbm.1), custom_call_target="tpu_custom_call" | custom-call | tf_op jit(solution)/shard_map/spread/pallas_call | solution.py:262
  1.1 0.0 copy-start
  1.1 0.0 copy-start.1
  1.2 16.3 %all_to_all.20.query_ref = bf16[32,8,128]{2,1,0:T(8,128)(2,1)S(1)} all-to-all(bf16[32,8,128]{2,1,0:T(8,128)(2,1)S(1)} %hold.1), channel_id=1, replica_groups={{176,144,168,184,208,112,136,152,160,200,216,240,16,80,104,120,128,192,..., dimensions={0} | all-to-all | bytes 131072 | tf_op jit(solution)/shard_map/all_to_all | solution.py:222
  17.4 0.0 copy-done
  17.4 0.0 copy-done.1
  17.4 0.0 copy-start.2
  17.4 2.1 %attention.1 = bf16[32,40,128]{2,1,0:T(8,128)(2,1)S(1)} custom-call(s32[32]{0:T(128)S(4)} %get-tuple-element.8.code_ref, bf16[32,8,128]{2,1,0:T(8,128)(2,1)S(1)} %all_to_all.20.query_ref, f32[2,32,8,128]{3,2,1,0:T(8,128)S(1)} %get-tuple-element.10.own_ref, bf16[32,512,128]{2,1,0:T(8,128)(2,1)S(1)} %copy-done, bf16[32,512,128]{2,1,0:T(8,128)(2,1)S(1)} %copy-done.1), custom_call_target="tpu_custom_call" | custom-call | tf_op jit(solution)/shard_map/attention/pallas_call | solution.py:286
  19.5 15.8 %all_to_all.21.parts_ref = bf16[32,40,128]{2,1,0:T(8,128)(2,1)S(1)} all-to-all(bf16[32,40,128]{2,1,0:T(8,128)(2,1)S(1)} %attention.1), channel_id=1, replica_groups={{176,144,168,184,208,112,136,152,160,200,216,240,16,80,104,120,128,192,..., dimensions={0} | all-to-all | bytes 655360 | tf_op jit(solution)/shard_map/all_to_all | solution.py:222
  35.3 0.3 finish.1
  35.7 6.7 %all_to_all.22.attended_ref = bf16[8,32,128]{2,1,0:T(8,128)(2,1)S(1)} all-to-all(bf16[8,32,128]{2,1,0:T(8,128)(2,1)S(1)} %finish.1), channel_id=1, replica_groups={{48,56,32,40,16,24,0,8},{112,120,96,104,80,88,64,72},{176,184,160,168,1..., dimensions={0} | all-to-all | bytes 131072 | tf_op jit(solution)/shard_map/all_to_all | solution.py:222
  42.4 0.0 copy-done.2
  42.4 0.3 project.1
  42.7 11.6 %all_to_all.23.terms_ref = f32[8,8,128]{2,1,0:T(8,128)S(1)} all-to-all(f32[8,8,128]{2,1,0:T(8,128)S(1)} %project.1), channel_id=1, replica_groups={{4,5,6,7,0,1,2,3},{12,13,14,15,8,9,10,11},{20,21,22,23,16,17,18,19},{28..., dimensions={0} | all-to-all | bytes 65536 | tf_op jit(solution)/shard_map/all_to_all | solution.py:222
  54.3 0.7 %sum.1 = bf16[32,32]{1,0:T(8,128)(2,1)} custom-call(f32[8,8,128]{2,1,0:T(8,128)S(1)} %all_to_all.23.terms_ref), custom_call_target="tpu_custom_call" | custom-call | tf_op jit(solution)/shard_map/sum/pallas_call | solution.py:313
  (1 shorter events, 0.0 us)
Async XLA Ops:
  1.1 16.3 %copy-start = (bf16[32,512,128]{2,1,0:T(8,128)(2,1)S(1)}, bf16[32,512,128]{2,1,0:T(8,128)(2,1)}, u32[]{:S(2)}) copy-start(bf16[32,512,128]{2,1,0:T(8,128)(2,1)} %key_ref.1) | copy-start | bytes 12582916
  1.1 16.3 %copy-start.1 = (bf16[32,512,128]{2,1,0:T(8,128)(2,1)S(1)}, bf16[32,512,128]{2,1,0:T(8,128)(2,1)}, u32[]{:S(2)}) copy-start(bf16[32,512,128]{2,1,0:T(8,128)(2,1)} %value_ref.1) | copy-start | bytes 12582916
  17.4 25.0 %copy-start.2 = (bf16[1024,256]{1,0:T(8,128)(2,1)S(1)}, bf16[1024,256]{1,0:T(8,128)(2,1)}, u32[]{:S(2)}) copy-start(bf16[1024,256]{1,0:T(8,128)(2,1)} %w_ref.1) | copy-start | bytes 1572868
